TPU v7x, 32 devices: a whole 2x2x4 slice. The times are simulated.
32 devices in a mesh: lon: 8 (over z, x), lat: 4 (over y, core).
Axes of the slice: x: 2, y: 2, z: 4, core: 2. Of those that a mesh axis runs over, the one named last changes fastest.
Arguments:
- tokens: bfloat16 [4, 24, 192, 192], P(None, 'lat', 'lon'), may hold values from -6 to 6
- cotangent: bfloat16 [4, 24, 192, 192], P(None, 'lat', 'lon'), may hold values from -6 to 6
- land_sea: int32 [24, 192], P('lat', 'lon'), may hold values 0 or 1
- land_vector: float32 [192], replicated, may hold values from -4 to 4
- triple_weight: bfloat16 [192, 576], replicated, may hold values from -0.4375 to 0.4375
- project_weight: bfloat16 [192, 192], replicated, may hold values from -0.4375 to 0.4375
- up_weight: bfloat16 [192, 768], replicated, may hold values from -0.4375 to 0.4375
- down_weight: bfloat16 [768, 192], replicated, may hold values from -0.21875 to 0.21875
- earth_bias: float32 [4, 2, 6, 144, 23], P('lat'), may hold values from -5 to 5
Outputs:
- grad_tokens: bfloat16 [4, 24, 192, 192], P(None, 'lat', 'lon')
- grad_triple: float32 [192, 576], replicated
- grad_project: float32 [192, 192], replicated
- grad_up: float32 [192, 768], replicated
- grad_down: float32 [768, 192], replicated
- grad_land: float32 [192], replicated
All inputs are finite; a program needn't handle non-finite values. No bound on the sum of `land_sea` on one device may be relied on, other than what follows from the above.
Results may differ from a plain program's by a relative error of at most 0.013.
Values may be sent and summed in bfloat16 or wider, within the bound.
No kernel may reach another device: no remote copies, remote signals or barrier semaphores. Data moves between devices by JAX's collectives and lax.ppermute only.
A program may use at most 128 MiB of HBM per device.

v0:
```python
import functools
import math

import jax
import jax.numpy as jnp
import numpy as np
from jax import lax
from jax.experimental import pallas as pl
from jax.experimental.pallas import tpu as pltpu
from jax.sharding import PartitionSpec as P

Z = 4
WZ = 2
WH = 6
WW = 12
C = 192
HEADS = 6
HEAD = 32
FF = 768
HZ, HH, HW = WZ // 2, WH // 2, WW // 2
TOK = WZ * WH * WW
PLACES = WZ * WH
RELW = 2 * WW - 1
SPOTS = PLACES // 2
STRIP = -(-RELW * SPOTS // 128) * 128
RUN, SHORT = WW * SPOTS, (WW - HW) * SPOTS

mask_fill = -10000.0
norm_eps = 1e-05
log2e = 1.4426950408889634
root_half = 0.7071067811865476
inv_root_tau = 0.3989422804014327
score_scale = HEAD**-0.5

f32 = jnp.float32
bf16 = jnp.bfloat16
MIB = 1 << 20

QUADS = 4
PART = C // (2 * QUADS)
CHUNK = 3 * PART
BLOCKS = FF // 128
EXTRA = 8
FULL = BLOCKS * CHUNK + EXTRA
FIRST = FULL // 16 * 8


def mm(a, b):
    return lax.dot_general(a, b, (((1,), (0,)), ((), ())), preferred_element_type=f32)


def mm_nt(a, b):
    return lax.dot_general(a, b, (((1,), (1,)), ((), ())), preferred_element_type=f32)


def mm_tn(a, b):
    return lax.dot_general(a, b, (((0,), (0,)), ((), ())), preferred_element_type=f32)


def unit_norm(values):
    average = jnp.mean(values, -1, keepdims=True)
    centred = values - average
    variance = jnp.mean(centred * centred, -1, keepdims=True)
    spread = lax.rsqrt(variance + norm_eps)
    return centred * spread, spread


def norm_back(upstream, unit, spread):
    first = jnp.mean(upstream, -1, keepdims=True)
    second = jnp.mean(upstream * unit, -1, keepdims=True)
    return spread * (upstream - first - unit * second)


def piece_rows(rows, cols):
    home = np.arange(Z * rows * cols).reshape(Z, rows, cols)

    def run(level, row, col, width):
        levels = [(level * WZ + z - HZ) % Z for z in range(WZ)]
        return home[levels, row : row + HH, col : col + width].transpose(2, 0, 1).reshape(-1)

    levels = range(Z // WZ)
    parts = []
    for row in (0, rows - HH):
        whole = [run(a, row, w * WW - HW, WW) for w in range(1, cols // WW) for a in levels]
        parts.append(np.concatenate(whole + [run(a, row, 0, WW - HW) for a in levels]))
    for row in (0, rows - HH):
        parts.append(np.concatenate([run(a, row, cols - HW, HW) for a in levels]))
    return parts


def window_runs(lon_windows):
    levels = Z // WZ
    whole = (lon_windows - 1) * levels
    runs = [[(1, n * RUN, RUN), (0, n * RUN, RUN)] for n in range(whole)]
    for a in range(levels):
        inner = whole * RUN + a * SHORT
        west = (a * (RUN - SHORT), RUN - SHORT)
        runs.append([(3, *west), (1, inner, SHORT), (2, *west), (0, inner, SHORT)])
    return runs


def spots(places):
    return jnp.asarray(np.argsort(places).astype(np.int32)[None])


def one_hot(spot_ref):
    count = spot_ref.shape[1]
    rows = lax.broadcasted_iota(jnp.int32, (count, count), 0)
    return (rows == spot_ref[...]).astype(f32).astype(bf16)


def vmem(count):
    return [pl.BlockSpec(memory_space=pltpu.VMEM)] * count


def shape(dims, dtype):
    return jax.ShapeDtypeStruct(dims, dtype)


def cost(flops, moved):
    return pl.CostEstimate(flops=flops, bytes_accessed=moved, transcendentals=0)


def land_column(land_ref, rows, cols):
    eye = (
        lax.broadcasted_iota(jnp.int32, (cols, cols), 0)
        == lax.broadcasted_iota(jnp.int32, (cols, cols), 1)
    ).astype(f32)
    land = land_ref[...].astype(f32)
    parts = [jnp.sum(eye * land[i : i + 1, :], -1, keepdims=True) for i in range(rows)]
    return jnp.concatenate(parts, axis=0)


def pack_kernel(rows, cols, *refs):
    sources, outs, (tokens_ref, cot_ref, land_ref, vec_ref, perm_ref, sems) = refs[:5], refs[5:-6], refs[-6:]
    copies = [
        pltpu.make_async_copy(source, target, sems.at[n])
        for n, (source, target) in enumerate(zip(sources, (tokens_ref, cot_ref, land_ref, vec_ref, perm_ref)))
    ]
    for copy in copies:
        copy.start()
    for copy in copies:
        copy.wait()
    column = land_column(land_ref, rows, cols)
    added = column * vec_ref[...]
    added = jnp.concatenate([added] * Z, axis=0)
    embedded = (tokens_ref[...].astype(f32) + added).astype(bf16)
    perm = one_hot(perm_ref)
    left = mm(perm, embedded)
    right = mm(perm, cot_ref[...])
    packed = jnp.concatenate([left, right], axis=1)
    start = 0
    for out in outs:
        out[...] = packed[start : start + out.shape[0]].astype(bf16)
        start += out.shape[0]


def pack(tokens, cotangent, land_sea, vector, rows, cols):
    parts = piece_rows(rows, cols)
    perm = spots(np.concatenate(parts))
    count = Z * rows * cols
    return pl.pallas_call(
        functools.partial(pack_kernel, rows, cols),
        out_shape=[shape((part.size, 2 * C), bf16) for part in parts],
        in_specs=[pl.BlockSpec(memory_space=pltpu.HBM)] * 5,
        out_specs=vmem(4),
        scratch_shapes=[
            pltpu.VMEM((count, C), bf16),
            pltpu.VMEM((count, C), bf16),
            pltpu.VMEM((rows, cols), jnp.int32),
            pltpu.VMEM((1, C), f32),
            pltpu.VMEM((1, count), jnp.int32),
            pltpu.SemaphoreType.DMA((5,)),
        ],
        cost_estimate=cost(4 * count * count * C, 4 * MIB),
        name="pack",
    )(tokens.reshape(count, C), cotangent.reshape(count, C), land_sea, vector.reshape(1, C), perm)


def floor_div(values, divisor):
    return (values * (65536 // divisor + 1)) >> 16


def remainder(values, divisor):
    return values - floor_div(values, divisor) * divisor


def place_order(order):
    half = floor_div(order, SPOTS)
    spot = order - half * SPOTS
    level = floor_div(spot, HH)
    return level * WH + half * HH + (spot - level * HH)


def bias_kernel(levels, table_ref, out_ref, *wide_refs):
    groups = levels * HEADS
    pairs = PLACES * PLACES
    row = lax.broadcasted_iota(jnp.int32, (HEADS * RELW, HEADS * STRIP), 0)
    lane = lax.broadcasted_iota(jnp.int32, (HEADS * RELW, HEADS * STRIP), 1)
    head = floor_div(row, RELW)
    ahead = lane - (head * STRIP + (RELW - 1 - (row - head * RELW)) * SPOTS)
    onehot = ((ahead >= 0) & (ahead < SPOTS)).astype(f32).astype(bf16)
    row = lax.broadcasted_iota(jnp.int32, (pairs, pairs), 0)
    source = place_order(floor_div(row, PLACES)) * PLACES + remainder(row, PLACES)
    reorder = (lax.broadcasted_iota(jnp.int32, (pairs, pairs), 1) == source).astype(f32).astype(bf16)
    for level in range(levels):
        table = table_ref[:, level, :].T
        high = table.astype(bf16)
        rest = (table - high.astype(f32)).astype(bf16)
        wide = mm(mm(reorder, high).astype(bf16), onehot) + mm(mm(reorder, rest).astype(bf16), onehot)
        for head in range(HEADS):
            for n, wide_ref in enumerate(wide_refs):
                start = head * STRIP + n * 128
                wide_ref[(level * HEADS + head) * pairs : (level * HEADS + head + 1) * pairs, :] = wide[:, start : start + 128]
    strips = groups * PLACES
    row = lax.broadcasted_iota(jnp.int32, (strips, STRIP), 0)
    spot = remainder(lax.broadcasted_iota(jnp.int32, (strips, STRIP), 1), SPOTS)
    own = remainder(row, PLACES)
    first_level = (row < HEADS * PLACES).astype(jnp.int32)
    own_north = (own < SPOTS).astype(jnp.int32)
    own_low = (own - SPOTS * (1 - own_north) < HZ * HH).astype(jnp.int32)
    low = (spot < HZ * HH).astype(jnp.int32)
    pole = (lax.axis_index("y") + lax.axis_index("core") == 0).astype(jnp.int32)
    halves = []
    for half in range(2):
        parts = []
        for n, wide_ref in enumerate(wide_refs):
            here = spot[:, n * 128 : (n + 1) * 128]
            part = jnp.zeros((strips, 128), f32)
            for p in range(SPOTS):
                place = p // HH * WH + half * HH + p % HH
                part = jnp.where(here == p, wide_ref[pl.ds(place, strips, stride=PLACES), :], part)
            parts.append(part)
        strip = jnp.concatenate(parts, axis=1)
        differs = first_level * (own_low ^ low) + pole * (own_north ^ (1 - half))
        halves.append(jnp.where(differs > 0, strip + mask_fill, strip) * log2e)
    for w in range(WW):
        start = (WW - 1 - w) * SPOTS
        part = jnp.concatenate([strip[:, start : start + RUN] for strip in halves], axis=1)
        for g in range(groups):
            for half in range(2):
                rows = part[g * PLACES + half * SPOTS : g * PLACES + (half + 1) * SPOTS, :]
                out_ref[g, half * RUN + w * SPOTS : half * RUN + (w + 1) * SPOTS, :] = rows


def expand_bias(table):
    levels = table.shape[1]
    groups = levels * HEADS
    pairs = PLACES * PLACES
    flat = table[0].transpose(1, 3, 0, 2).reshape(HEADS * RELW, levels, pairs)
    return pl.pallas_call(
        functools.partial(bias_kernel, levels),
        out_shape=shape((groups, TOK, TOK), f32),
        in_specs=vmem(1),
        out_specs=vmem(1)[0],
        scratch_shapes=[pltpu.VMEM((groups * pairs, 128), f32)] * (STRIP // 128),
        compiler_params=pltpu.CompilerParams(vmem_limit_bytes=28 * MIB),
        cost_estimate=cost(10**9, 8 * MIB),
        name="bias",
    )(flat)


def head_masks(count):
    lane = lax.broadcasted_iota(jnp.int32, (count, C), 1)
    return [((lane >= h * HEAD) & (lane < (h + 1) * HEAD)).astype(f32) for h in range(HEADS)]


def stacked(values, masks):
    return jnp.concatenate([values * mask for mask in masks], axis=0)


def head_sum(values, masks):
    total = values[:TOK] * masks[0]
    for h in range(1, HEADS):
        total = total + values[h * TOK : (h + 1) * TOK] * masks[h]
    return total


def position():
    return lax.axis_index("core"), lax.axis_index("y") * 2 + lax.axis_index("x"), lax.axis_index("deep")


def chunk_rows(block):
    return pl.ds(pl.multiple_of(block * PART, PART), PART)


def split_parts(total_refs, keep_ref, send_ref):
    core, chip, _ = position()
    for out, side in ((keep_ref, core), (send_ref, 1 - core)):
        parts = []
        for g in range(QUADS):
            rows = chunk_rows(side * QUADS + jnp.bitwise_xor(chip, g))
            parts += [ref[rows, :] for ref in total_refs]
        out[...] = jnp.concatenate(parts, axis=0).astype(out.dtype)


def forward_kernel(
    windows, lon_windows,
    own_ref, north_ref, side_ref, corner_ref, bias_ref, triple_ref, project_ref, up_ref, down_ref,
    q_ref, k_ref, v_ref, p_ref, mixed_ref, normed_ref, unit_ref, spread_ref, gsum_ref, up_grad_ref, down_grad_ref,
    branch_ref, cot_ref, emb_ref,
):
    pieces = [ref[...].astype(f32) for ref in (own_ref, north_ref, side_ref, corner_ref)]
    runs = [run for window in window_runs(lon_windows) for run in window]
    ordered = jnp.concatenate([pieces[n][start : start + count] for n, start, count in runs], axis=0)
    emb = ordered[:, :C]
    emb_ref[...] = emb
    cot_ref[...] = ordered[:, C:].astype(bf16)
    unit, spread = unit_norm(emb)
    unit_ref[...] = unit
    spread_ref[...] = spread
    normed = unit.astype(bf16)
    normed_ref[...] = normed
    packed = mm(normed, triple_ref[...])
    q_ref[...] = packed[:, :C].astype(bf16)
    k_ref[...] = packed[:, C : 2 * C].astype(bf16)
    v_ref[...] = packed[:, 2 * C :].astype(bf16)
    masks = head_masks(TOK)
    masks_b = [mask.astype(bf16) for mask in masks]

    def window_step(w, carry):
        rows = pl.ds(pl.multiple_of(w * TOK, TOK), TOK)
        level = w % (Z // WZ)
        scores = mm_nt(stacked(q_ref[rows, :], masks_b), k_ref[rows, :])
        bias = bias_ref[pl.ds(level * HEADS, HEADS)].reshape(HEADS * TOK, TOK)
        raised = jnp.exp2(scores * (score_scale * log2e) + bias)
        probs = raised * (1.0 / jnp.sum(raised, -1, keepdims=True))
        probs_b = probs.astype(bf16)
        p_ref[pl.ds(w * HEADS, HEADS)] = probs_b.reshape(HEADS, TOK, TOK)
        mixed = head_sum(mm(probs_b, v_ref[rows, :]), masks).astype(bf16)
        mixed_ref[rows, :] = mixed
        branch_ref[rows, :] = mm(mixed, project_ref[...])
        return carry

    lax.fori_loop(0, windows, window_step, 0, unroll=True)

    attended = branch_ref[...].astype(bf16).astype(f32)
    unit2, spread2 = unit_norm(emb_ref[...] + attended)
    normed2 = unit2.astype(bf16)
    cot = cot_ref[...]
    back = jnp.zeros(unit2.shape, f32)
    block = 256
    for start in range(0, FF, block):
        cols = slice(start, start + block)
        up_part = up_ref[:, cols]
        pre = mm(normed2, up_part)
        upstream = mm(cot, down_ref[:, cols])
        phi = 0.5 * (1.0 + lax.erf(pre * root_half))
        activated = (pre * phi).astype(bf16)
        slope = phi + pre * inv_root_tau * jnp.exp2(pre * pre * (-0.5 * log2e))
        hidden = (upstream * slope).astype(bf16)
        up_grad_ref[:, cols] = mm_tn(normed2, hidden)
        down_grad_ref[:, cols] = mm_tn(cot, activated)
        back = back + mm_nt(hidden, up_part)
    gsum_ref[...] = cot.astype(f32) + norm_back(back, unit2, spread2)


def windows_back_kernel(windows, q_ref, k_ref, v_ref, p_ref, gsum_ref, project_ref, gq_ref, gk_ref, gv_ref):
    masks = head_masks(TOK)
    masks_b = [mask.astype(bf16) for mask in masks]

    def window_step(w, carry):
        rows = pl.ds(pl.multiple_of(w * TOK, TOK), TOK)
        grad = gsum_ref[rows, :].astype(bf16)
        grad_mixed = mm_nt(grad, project_ref[...])
        grad_mixed_b = grad_mixed.astype(bf16)
        probs_b = p_ref[pl.ds(w * HEADS, HEADS)].reshape(HEADS * TOK, TOK)
        probs = probs_b.astype(f32)
        grad_probs = mm_nt(stacked(grad_mixed_b, masks_b), v_ref[rows, :])
        inner = jnp.sum(grad_probs * probs, -1, keepdims=True)
        scaled = (probs * (grad_probs - inner) * score_scale).astype(bf16)
        grad_q = head_sum(mm(scaled, k_ref[rows, :]), masks)
        grad_mixed_t = grad_mixed_b.astype(f32).T.astype(bf16)
        query_t = q_ref[rows, :].astype(f32).T.astype(bf16)
        grad_k, grad_v = [], []
        for h in range(HEADS):
            spot = slice(h * HEAD, (h + 1) * HEAD)
            span = slice(h * TOK, (h + 1) * TOK)
            grad_k.append(mm(query_t[spot], scaled[span]))
            grad_v.append(mm(grad_mixed_t[spot], probs_b[span]))
        gq_ref[rows, :] = grad_q.astype(bf16)
        gk_ref[rows, :] = jnp.concatenate(grad_k, axis=0).T.astype(bf16)
        gv_ref[rows, :] = jnp.concatenate(grad_v, axis=0).T.astype(bf16)
        return carry

    lax.fori_loop(0, windows, window_step, 0, unroll=True)


def halved(rows):
    return -(-rows // 16) * 8


def tokens_back_kernel(
    lon_windows, sizes, gq_ref, gk_ref, gv_ref, mixed_ref, normed_ref, unit_ref, spread_ref, gsum_ref, triple_ref,
    up_grad_ref, down_grad_ref, *rest,
):
    outs, (keep_ref, send_ref, total_ref) = rest[: len(sizes)], rest[len(sizes) :]
    normed = normed_ref[...]
    triple = triple_ref[...]
    grad_normed = jnp.zeros(unit_ref.shape, f32)
    parts = []
    for n, ref in enumerate((gq_ref, gk_ref, gv_ref)):
        grad = ref[...]
        grad_normed = grad_normed + mm_nt(grad, triple[:, n * C : (n + 1) * C])
        parts.append(mm_tn(normed, grad))
    parts.append(mm_tn(mixed_ref[...], gsum_ref[...].astype(bf16)))
    total_ref[...] = jnp.concatenate(parts, axis=1)
    grad_normed = grad_normed.astype(bf16).astype(f32)
    grad_tokens = gsum_ref[...] + norm_back(grad_normed, unit_ref[...], spread_ref[...])
    parts, at = [[] for _ in sizes], 0
    for n, start, count in [run for window in window_runs(lon_windows) for run in window]:
        parts[n].append((start, grad_tokens[at : at + count]))
        at += count
    for size, out, part in zip(sizes, outs, parts):
        piece = jnp.concatenate([value for _, value in sorted(part, key=lambda item: item[0])], axis=0)
        half = halved(size)
        second = jnp.concatenate([piece[half:], jnp.zeros((2 * half - size, C), f32)], axis=0)
        out[...] = jnp.concatenate([piece[:half], second], axis=1).astype(bf16)
    split_parts((up_grad_ref, down_grad_ref, total_ref), keep_ref, send_ref)


def block_kernel(windows, lon_windows, sizes, *refs):
    ins, refs = refs[:9], refs[9:]
    pieces, (bias_ref, triple_ref, project_ref, up_ref, down_ref) = ins[:4], ins[4:]
    outs, refs = refs[: len(sizes) + 2], refs[len(sizes) + 2 :]
    q, k, v, p, mixed, normed, unit, spread, gsum, up_grad, down_grad, branch, cot, emb, gq, gk, gv, total = refs
    forward_kernel(
        windows, lon_windows, *pieces, bias_ref, triple_ref, project_ref, up_ref, down_ref,
        q, k, v, p, mixed, normed, unit, spread, gsum, up_grad, down_grad, branch, cot, emb,
    )
    windows_back_kernel(windows, q, k, v, p, gsum, project_ref, gq, gk, gv)
    tokens_back_kernel(
        lon_windows, sizes, gq, gk, gv, mixed, normed, unit, spread, gsum, triple_ref, up_grad, down_grad, *outs, total
    )


def block(pieces, bias, triple, project, up, down, lon_windows, sizes):
    count = sum(sizes)
    windows = count // TOK
    out_shape = [shape((halved(size), 2 * C), bf16) for size in sizes] + [
        shape((QUADS * CHUNK, FF), f32),
        shape((QUADS * CHUNK, FF), bf16),
    ]
    rows = [pltpu.VMEM((count, C), dtype) for dtype in (bf16, f32)]
    return pl.pallas_call(
        functools.partial(block_kernel, windows, lon_windows, sizes),
        out_shape=out_shape,
        in_specs=vmem(9),
        out_specs=vmem(len(out_shape)),
        scratch_shapes=rows[:1] * 3
        + [pltpu.VMEM((windows * HEADS, TOK, TOK), bf16)]
        + rows[:1] * 2
        + [rows[1], pltpu.VMEM((count, 1), f32), rows[1]]
        + [pltpu.VMEM((C, FF), f32)] * 2
        + [rows[1], rows[0], rows[1]]
        + rows[:1] * 3
        + [pltpu.VMEM((C, FF), f32)],
        compiler_params=pltpu.CompilerParams(vmem_limit_bytes=32 * MIB),
        cost_estimate=cost(8 * 10**9, 16 * MIB),
        name="block",
    )(*pieces, bias, triple, project, up, down)


def home_kernel(sizes, rows, cols, own_ref, north_ref, side_ref, corner_ref, perm_ref, land_ref, out_ref, sum_ref):
    pieces = []
    for size, ref in zip(sizes, (own_ref, north_ref, side_ref, corner_ref)):
        wide = ref[...].astype(f32)
        pieces += [wide[:, :C], wide[: size - wide.shape[0], C:]]
    pieces = jnp.concatenate(pieces, axis=0).astype(bf16)
    grads = mm(one_hot(perm_ref), pieces)
    out_ref[...] = grads.astype(bf16)
    column = jnp.concatenate([land_column(land_ref, rows, cols)] * Z, axis=0)
    sum_ref[...] = jnp.sum(grads * column, 0, keepdims=True)


def to_home(pieces, land_sea, sizes, rows, cols):
    count = Z * rows * cols
    perm = spots(np.argsort(np.concatenate(piece_rows(rows, cols))))
    return pl.pallas_call(
        functools.partial(home_kernel, sizes, rows, cols),
        out_shape=[shape((count, C), bf16), shape((1, C), f32)],
        in_specs=vmem(6),
        out_specs=vmem(2),
        compiler_params=pltpu.CompilerParams(vmem_limit_bytes=32 * MIB),
        cost_estimate=cost(2 * count * count * C, 4 * MIB),
        name="to_home",
    )(*pieces, perm, land_sea)


def core_add_kernel(keep_ref, got_ref, *refs):
    own_ref, outs = refs[-QUADS], refs[1 - QUADS :]
    total = keep_ref[...] + got_ref[...].astype(f32)
    own_ref[...] = total[:CHUNK]
    for e, out in enumerate(outs, 1):
        out[...] = total[e * CHUNK : (e + 1) * CHUNK].astype(bf16)


def chip_add_kernel(keep_ref, *refs):
    gots, (land_ref, first_ref, second_ref) = refs[:-3], refs[-3:]
    total = keep_ref[...]
    for ref in gots:
        total = total + ref[...].astype(f32)
    land = land_ref[...]
    rest = jnp.concatenate([land[:, 128:], jnp.zeros((1, 2 * 128 - C), f32)], axis=1)
    parts = [total[:, n * 128 : (n + 1) * 128] for n in range(BLOCKS)]
    total = jnp.concatenate(parts + [land[:, :128], rest, jnp.zeros((EXTRA - 2, 128), f32)], axis=0)
    first_ref[...] = total[:FIRST].astype(bf16)
    second_ref[...] = total[FIRST:].astype(bf16)


def add_kernel(one_ref, two_ref, out_ref):
    out_ref[...] = (one_ref[...].astype(f32) + two_ref[...].astype(f32)).astype(bf16)


def join_kernel(*refs):
    refs[-1][...] = jnp.concatenate([ref[...] for ref in refs[:-1]], axis=0)


def small_call(kernel, out_shape, args, name, after=(), scratch=()):
    return pl.pallas_call(
        kernel,
        out_shape=out_shape,
        in_specs=vmem(len(args)) + [pl.BlockSpec(memory_space=pl.ANY)] * len(after),
        out_specs=vmem(len(out_shape)),
        scratch_shapes=scratch,
        compiler_params=pltpu.CompilerParams(vmem_limit_bytes=16 * MIB),
        cost_estimate=cost(10**6, 2 * MIB),
        name=name,
    )(*args, *after)


def finish_kernel(far, chunks_ref, *refs):
    if far:
        before_ref, refs = refs[0], refs[5:]
    outs, land_ref, (up_ref, down_ref, triple_ref, project_ref, lands_ref, sum_ref, sems) = refs[:4], refs[4], refs[5:]
    core, chip, _ = position()
    side = 1 - core if far else core
    for g in range(QUADS):
        tiles = chunks_ref[g * FULL : (g + 1) * FULL, :].astype(f32)
        chunk = jnp.concatenate([tiles[n * CHUNK : (n + 1) * CHUNK] for n in range(BLOCKS)], axis=1)
        block = jnp.bitwise_xor(chip, g)
        rows = chunk_rows(block)
        up_ref[rows, :] = chunk[:PART]
        down_ref[rows, :] = chunk[PART : 2 * PART]
        triple_ref[rows, :] = chunk[2 * PART : CHUNK, : 3 * C]
        project_ref[rows, :] = chunk[2 * PART : CHUNK, 3 * C :]
        lands_ref[pl.ds(pl.multiple_of(block * EXTRA, EXTRA), EXTRA), :] = tiles[BLOCKS * CHUNK :]
    copies = []
    for n, (source, out) in enumerate(zip((triple_ref, project_ref, up_ref, down_ref), outs)):
        rows = pl.ds(pl.multiple_of(side * QUADS * PART, 8), QUADS * PART)
        copies.append(pltpu.make_async_copy(source, out.at[rows, :], sems.at[n]))
    for copy in copies:
        copy.start()
    lands = lands_ref[...]
    lands = [sum(lands[g * EXTRA + n : g * EXTRA + n + 1] for g in range(QUADS)) for n in range(2)]
    land = jnp.concatenate([lands[0], lands[1][:, : C - 128]], axis=1)
    if far:
        sum_ref[...] = land + before_ref[...]
        copies.append(pltpu.make_async_copy(sum_ref, land_ref, sems.at[4]))
        copies[-1].start()
    else:
        land_ref[...] = land
    for copy in copies:
        copy.wait()


def finish(chunks, before=()):
    rows = QUADS * PART
    widths = (3 * C, C, FF, FF)
    hbm = [pl.BlockSpec(memory_space=pltpu.HBM)] * 4
    land, weights = before[4:], before[:4]
    return pl.pallas_call(
        functools.partial(finish_kernel, bool(before)),
        out_shape=[shape((C, width), f32) for width in widths] + [shape((1, C), f32)],
        in_specs=vmem(1 + len(land)) + hbm[: len(weights)],
        out_specs=hbm + (hbm[:1] if before else vmem(1)),
        scratch_shapes=[
            pltpu.VMEM((rows, FF), f32),
            pltpu.VMEM((rows, FF), f32),
            pltpu.VMEM((rows, 3 * C), f32),
            pltpu.VMEM((rows, C), f32),
            pltpu.VMEM((QUADS * EXTRA, 128), f32),
            pltpu.VMEM((1, C), f32),
            pltpu.SemaphoreType.DMA((5,)),
        ],
        input_output_aliases={2 + n: n for n in range(len(weights))},
        compiler_params=pltpu.CompilerParams(vmem_limit_bytes=16 * MIB),
        cost_estimate=cost(10**6, 2 * MIB),
        name="finish_far" if before else "finish_own",
    )(chunks, *land, *weights)


def reduce_all(keep, sent, land, shift, lon_count, after):
    core_move = lambda lon, lat: (lon, lat ^ 1)
    chip_move = lambda e: lambda lon, lat: (lon ^ (e & 1), lat ^ (2 * (e >> 1)))
    deep_move = lambda e: lambda lon, lat: (lon ^ (2 * e), lat)

    def one(rows):
        return [shape((rows, FF), bf16)]

    got = shift(sent, move=core_move)
    parts = [shape((CHUNK, FF), f32)] + one(CHUNK) * (QUADS - 1)
    own, *parts = small_call(core_add_kernel, parts, (keep, got), "core_add", after=after)
    gots = [shift(value, move=chip_move(e)) for e, value in enumerate(parts, 1)]
    sides = [shape((rows, 128), bf16) for rows in (FIRST, FULL - FIRST)]
    totals = small_call(chip_add_kernel, sides, (own, *gots, land), "chip_add")
    steps = [(1, 3), (2, 1)]
    while 2 ** len(steps) < lon_count // 2:
        steps.append((2 ** len(steps),) * 2)
    for step in steps:
        gots = [shift(total, move=deep_move(e)) for total, e in zip(totals, step)]
        totals = [
            small_call(add_kernel, [side], pair, "deep_add")[0] for side, pair in zip(sides, zip(totals, gots))
        ]
    (total,) = small_call(join_kernel, [shape((FULL, 128), bf16)], totals, "deep_join")
    near = [total] + [shift(total, move=chip_move(e)) for e in range(1, QUADS)]
    (total,) = small_call(join_kernel, [shape((QUADS * FULL, 128), bf16)], near, "join")
    got = shift(total, move=core_move)
    return finish(got, finish(total))


AXES = ("deep", "x", "y", "core")


def send(value, lon_count, lat_count, move):
    pairs = []
    for lon in range(lon_count):
        for lat in range(lat_count):
            to_lon, to_lat = move(lon, lat)
            pairs.append((lon * lat_count + lat, (to_lon % lon_count) * lat_count + to_lat % lat_count))
    return lax.ppermute(value, AXES, pairs)


def body(
    lon_count, lat_count,
    tokens, cotangent, land_sea, land_vector, triple_weight, project_weight, up_weight, down_weight, earth_bias,
):
    levels, rows, cols, features = tokens.shape
    shift = functools.partial(send, lon_count=lon_count, lat_count=lat_count)
    lon_windows = cols // WW

    own, north, side, corner = pack(tokens, cotangent, land_sea, land_vector, rows, cols)
    north = shift(north, move=lambda lon, lat: (lon, lat + 1))
    side = shift(side, move=lambda lon, lat: (lon + 1, lat))
    corner = shift(corner, move=lambda lon, lat: (lon + 1, lat + 1))
    bias = expand_bias(earth_bias)

    sizes = [part.size for part in piece_rows(rows, cols)]
    pieces = (own, north, side, corner)
    own, north, side, corner, keep, sent = block(
        pieces, bias, triple_weight, project_weight, up_weight, down_weight.T, lon_windows, sizes
    )
    north = shift(north, move=lambda lon, lat: (lon, lat - 1))
    side = shift(side, move=lambda lon, lat: (lon - 1, lat))
    corner = shift(corner, move=lambda lon, lat: (lon - 1, lat - 1))
    after = (north, side, corner)
    grad_tokens, land = to_home((own, north, side, corner), land_sea, sizes, rows, cols)
    triple, project, up, down, land = reduce_all(keep, sent, land, shift, lon_count, after)
    return grad_tokens.reshape(tokens.shape), triple, project, up, down.T, land.reshape(features)


def solution(mesh):
    lon_count, lat_count = mesh.shape["lon"], mesh.shape["lat"]
    fine = jax.sharding.Mesh(mesh.devices.reshape(lon_count // 2, 2, lat_count // 2, 2), AXES)
    lon, lat = AXES[:2], AXES[2:]
    return jax.shard_map(
        functools.partial(body, lon_count, lat_count),
        mesh=fine,
        in_specs=(
            P(None, lat, lon, None),
            P(None, lat, lon, None),
            P(lat, lon),
            P(),
            P(),
            P(),
            P(),
            P(),
            P(lat, None, None, None, None),
        ),
        out_specs=(P(None, lat, lon, None), P(), P(), P(), P(), P()),
        check_vma=False,
    )
```

profile of v0, /device:TPU:0, one launch (start us, length us, event | category | flops | bytes accessed | tf_op | source)
XLA Modules:
  0.0 62.1 jit_solution(17608253048761496698)
XLA Ops:
  0.6 2.6 %pack.1 = (bf16[216,384]{1,0:T(8,128)(2,1)}, bf16[216,384]{1,0:T(8,128)(2,1)}, bf16[72,384]{1,0:T(8,128)(2,1)}, bf16[72,384]{1,0:T(8,128)(2,1)}) custom-call(bf16[576,192]{1,0:T(8,128)(2,1)} %bitcast.15, bf16[576,192]{1,0:T(8,128)(2,1)} %bitcast.16, s32[6,24]{1,0:T(8,128)} %land_ref.1, f32[1,192]{1,0:T(1,128)} %bitcast.17, s32[1,576]{1,0:T(1,128)} %constant.4.clone.refs_4_), custom_call_target="tpu_custom_call" | custom-call | flops 254803968 | bytes 4194304 | tf_op jit(solution)/shard_map/pack/pallas_call | solution.py:162
  3.2 0.5 collective-permute-start
  3.7 2.6 %collective-permute-start.1 = (bf16[72,384]{1,0:T(8,128)(2,1)}, bf16[72,384]{1,0:T(8,128)(2,1)S(1)}, u32[]{:S(2)}, u32[]{:S(2)}) collective-permute-start(bf16[72,384]{1,0:T(8,128)(2,1)} %get-tuple-element.36), channel_id=1, source_target_pairs={{0,4},{1,5},{2,6},{3,7},{4,8},{5,9},{6,10},{7,11},{8,12},{9,13},{1... | collective-permute-start | bytes 165896 | tf_op jit(solution)/shard_map/ppermute | solution.py:631
  6.3 2.4 %collective-permute-start.2 = (bf16[72,384]{1,0:T(8,128)(2,1)}, bf16[72,384]{1,0:T(8,128)(2,1)S(1)}, u32[]{:S(2)}, u32[]{:S(2)}) collective-permute-start(bf16[72,384]{1,0:T(8,128)(2,1)} %get-tuple-element.37), channel_id=1, source_target_pairs={{0,5},{1,6},{2,7},{3,4},{4,9},{5,10},{6,11},{7,8},{8,13},{9,14},{1... | collective-permute-start | bytes 165896 | tf_op jit(solution)/shard_map/ppermute | solution.py:631
  8.7 0.0 copy-start.2
  8.7 1.0 %copy-done.2 = f32[1,2,6,144,23]{3,1,4,2,0:T(2,128)S(1)} copy-done((f32[1,2,6,144,23]{3,1,4,2,0:T(2,128)S(1)}, f32[1,2,6,144,23]{3,1,4,2,0:T(2,128)}, u32[]{:S(2)}) %copy-start.2) | copy-done | bytes 159000
  9.7 0.0 copy-start
  9.7 0.0 copy-start.1
  9.7 0.0 copy-start.3
  9.7 0.0 copy-start.4
  9.7 0.0 copy-start.7
  9.7 1.4 %bias.1.refs_4_ = f32[12,144,144]{2,1,0:T(8,128)S(1)} custom-call(f32[138,2,144]{2,1,0:T(2,128)S(1)} %bitcast.13), custom_call_target="tpu_custom_call" | custom-call | flops 1000000000 | bytes 8388608 | tf_op jit(solution)/shard_map/bias/pallas_call | solution.py:251
  11.1 0.5 collective-permute-done.1.refs_2_
  11.7 2.2 %collective-permute-done.2.refs_3_ = bf16[72,384]{1,0:T(8,128)(2,1)S(1)} collective-permute-done((bf16[72,384]{1,0:T(8,128)(2,1)}, bf16[72,384]{1,0:T(8,128)(2,1)S(1)}, u32[]{:S(2)}, u32[]{:S(2)}) %collective-permute-start.2) | collective-permute-done | bytes 55328 | tf_op jit(solution)/shard_map/ppermute | solution.py:631
  13.8 0.0 collective-permute-done.refs_1_
  13.8 0.0 copy-done
  13.8 0.0 copy-done.1
  13.8 0.0 copy-done.3
  13.8 0.0 copy-done.4
  13.8 0.0 copy-done.7
  13.9 0.0 copy-start.5
  13.9 0.0 copy-start.6
  13.9 8.6 %block.1 = (bf16[112,384]{1,0:T(8,128)(2,1)S(1)}, bf16[112,384]{1,0:T(8,128)(2,1)S(1)}, bf16[40,384]{1,0:T(8,128)(2,1)S(1)}, bf16[40,384]{1,0:T(8,128)(2,1)S(1)}...) custom-call(bf16[216,384]{1,0:T(8,128)(2,1)S(1)} %copy-done.7, bf16[216,384]{1,0:T(8,128)(2,1)S(1)} %collective-permute-done.refs_1_, ...), custom_call_target="tpu_custom_call" | custom-call | flops 8000000000 | bytes 16777216 | tf_op jit(solution)/shard_map/block/pallas_call | solution.py:445
  22.5 0.4 collective-permute-start.6
  22.9 1.3 %collective-permute-start.3 = (bf16[112,384]{1,0:T(8,128)(2,1)S(1)}, bf16[112,384]{1,0:T(8,128)(2,1)S(1)}, u32[]{:S(2)}, u32[]{:S(2)}) collective-permute-start(bf16[112,384]{1,0:T(8,128)(2,1)S(1)} %get-tuple-element.39), channel_id=1, source_target_pairs={{0,3},{1,0},{2,1},{3,2},{4,7},{5,4},{6,5},{7,6},{8,11},{9,8},{10,9... | collective-permute-start | bytes 258056 | tf_op jit(solution)/shard_map/ppermute | solution.py:631
  24.2 1.6 %collective-permute-start.4 = (bf16[40,384]{1,0:T(8,128)(2,1)S(1)}, bf16[40,384]{1,0:T(8,128)(2,1)S(1)}, u32[]{:S(2)}, u32[]{:S(2)}) collective-permute-start(bf16[40,384]{1,0:T(8,128)(2,1)S(1)} %get-tuple-element.40), channel_id=1, source_target_pairs={{0,28},{1,29},{2,30},{3,31},{4,0},{5,1},{6,2},{7,3},{8,4},{9,5},{1... | collective-permute-start | bytes 92168 | tf_op jit(solution)/shard_map/ppermute | solution.py:631
  25.8 0.9 %collective-permute-start.5 = (bf16[40,384]{1,0:T(8,128)(2,1)S(1)}, bf16[40,384]{1,0:T(8,128)(2,1)S(1)}, u32[]{:S(2)}, u32[]{:S(2)}) collective-permute-start(bf16[40,384]{1,0:T(8,128)(2,1)S(1)} %get-tuple-element.41), channel_id=1, source_target_pairs={{0,31},{1,28},{2,29},{3,30},{4,3},{5,0},{6,1},{7,2},{8,7},{9,4},{1... | collective-permute-start | bytes 92168 | tf_op jit(solution)/shard_map/ppermute | solution.py:631
  26.7 1.4 %collective-permute-done.4.side_ref.refs_1_ = bf16[40,384]{1,0:T(8,128)(2,1)S(1)} collective-permute-done((bf16[40,384]{1,0:T(8,128)(2,1)S(1)}, bf16[40,384]{1,0:T(8,128)(2,1)S(1)}, u32[]{:S(2)}, u32[]{:S(2)}) %collective-permute-start.4) | collective-permute-done | bytes 30752 | tf_op jit(solution)/shard_map/ppermute | solution.py:631
  28.1 1.2 %collective-permute-done.5.corner_ref.refs_2_ = bf16[40,384]{1,0:T(8,128)(2,1)S(1)} collective-permute-done((bf16[40,384]{1,0:T(8,128)(2,1)S(1)}, bf16[40,384]{1,0:T(8,128)(2,1)S(1)}, u32[]{:S(2)}, u32[]{:S(2)}) %collective-permute-start.5) | collective-permute-done | bytes 30752 | tf_op jit(solution)/shard_map/ppermute | solution.py:631
  29.2 0.0 collective-permute-done.3.north_ref.refs_0_
  29.2 0.0 collective-permute-done.6.got_ref
  29.2 0.1 core_add.1
  29.3 1.4 %collective-permute-start.7 = (bf16[72,768]{1,0:T(8,128)(2,1)S(1)}, bf16[72,768]{1,0:T(8,128)(2,1)S(1)}, u32[]{:S(2)}, u32[]{:S(2)}) collective-permute-start(bf16[72,768]{1,0:T(8,128)(2,1)S(1)} %get-tuple-element.46), channel_id=1, source_target_pairs={{0,4},{1,5},{2,6},{3,7},{4,0},{5,1},{6,2},{7,3},{8,12},{9,13},{10,... | collective-permute-start | bytes 331784 | tf_op jit(solution)/shard_map/ppermute | solution.py:631
  30.7 0.7 %collective-permute-start.8 = (bf16[72,768]{1,0:T(8,128)(2,1)S(1)}, bf16[72,768]{1,0:T(8,128)(2,1)S(1)}, u32[]{:S(2)}, u32[]{:S(2)}) collective-permute-start(bf16[72,768]{1,0:T(8,128)(2,1)S(1)} %get-tuple-element.47), channel_id=1, source_target_pairs={{0,2},{1,3},{2,0},{3,1},{4,6},{5,7},{6,4},{7,5},{8,10},{9,11},{10,... | collective-permute-start | bytes 331784 | tf_op jit(solution)/shard_map/ppermute | solution.py:631
  31.3 1.5 %collective-permute-start.9 = (bf16[72,768]{1,0:T(8,128)(2,1)S(1)}, bf16[72,768]{1,0:T(8,128)(2,1)S(1)}, u32[]{:S(2)}, u32[]{:S(2)}) collective-permute-start(bf16[72,768]{1,0:T(8,128)(2,1)S(1)} %get-tuple-element.48), channel_id=1, source_target_pairs={{0,6},{1,7},{2,4},{3,5},{4,2},{5,3},{6,0},{7,1},{8,14},{9,15},{10,... | collective-permute-start | bytes 331784 | tf_op jit(solution)/shard_map/ppermute | solution.py:631
  32.9 0.0 copy-done.5
  32.9 0.0 copy-done.6
  32.9 1.2 %to_home.1 = (bf16[576,192]{1,0:T(8,128)(2,1)}, f32[1,192]{1,0:T(1,128)S(1)}) custom-call(bf16[112,384]{1,0:T(8,128)(2,1)S(1)} %get-tuple-element.38.own_ref, bf16[112,384]{1,0:T(8,128)(2,1)S(1)} %collective-permute-done.3.north_ref.refs_0_, bf16[40,384]{1,0:T(8,128)(2,1)S(1)} %collective-permute-done.4.side_ref.refs_1_, ...), custom_call_target="tpu_custom_call" | custom-call | flops 127401984 | bytes 4194304 | tf_op jit(solution)/shard_map/to_home/pallas_call | solution.py:479
  34.1 0.1 collective-permute-done.7.refs_0_
  34.1 3.7 %collective-permute-done.8.refs_1_ = bf16[72,768]{1,0:T(8,128)(2,1)S(1)} collective-permute-done((bf16[72,768]{1,0:T(8,128)(2,1)S(1)}, bf16[72,768]{1,0:T(8,128)(2,1)S(1)}, u32[]{:S(2)}, u32[]{:S(2)}) %collective-permute-start.8) | collective-permute-done | bytes 110624 | tf_op jit(solution)/shard_map/ppermute | solution.py:631
  37.8 0.0 collective-permute-done.9.refs_2_
  37.8 0.1 chip_add.1
  37.9 3.7 %collective-permute-start.12 = (bf16[224,128]{1,0:T(8,128)(2,1)S(1)}, bf16[224,128]{1,0:T(8,128)(2,1)S(1)}, u32[]{:S(2)}, u32[]{:S(2)}) collective-permute-start(bf16[224,128]{1,0:T(8,128)(2,1)S(1)} %get-tuple-element.51.one_ref), channel_id=1, source_target_pairs={{0,24},{1,25},{2,26},{3,27},{4,28},{5,29},{6,30},{7,31},{8,16},{9,... | collective-permute-start | bytes 172040 | tf_op jit(solution)/shard_map/ppermute | solution.py:631
  41.5 0.0 collective-permute-start.10
  41.5 2.4 %collective-permute-done.12.two_ref = bf16[224,128]{1,0:T(8,128)(2,1)S(1)} collective-permute-done((bf16[224,128]{1,0:T(8,128)(2,1)S(1)}, bf16[224,128]{1,0:T(8,128)(2,1)S(1)}, u32[]{:S(2)}, u32[]{:S(2)}) %collective-permute-start.12) | collective-permute-done | bytes 57376 | tf_op jit(solution)/shard_map/ppermute | solution.py:631
  43.9 0.1 collective-permute-start.13
  44.0 1.7 %collective-permute-done.10.two_ref = bf16[216,128]{1,0:T(8,128)(2,1)S(1)} collective-permute-done((bf16[216,128]{1,0:T(8,128)(2,1)S(1)}, bf16[216,128]{1,0:T(8,128)(2,1)S(1)}, u32[]{:S(2)}, u32[]{:S(2)}) %collective-permute-start.10) | collective-permute-done | bytes 55328 | tf_op jit(solution)/shard_map/ppermute | solution.py:631
  45.7 2.5 %collective-permute-start.11 = (bf16[216,128]{1,0:T(8,128)(2,1)S(1)}, bf16[216,128]{1,0:T(8,128)(2,1)S(1)}, u32[]{:S(2)}, u32[]{:S(2)}) collective-permute-start(bf16[216,128]{1,0:T(8,128)(2,1)S(1)} %deep_add.4.one_ref), channel_id=1, source_target_pairs={{0,16},{1,17},{2,18},{3,19},{4,20},{5,21},{6,22},{7,23},{8,24},{9,... | collective-permute-start | bytes 165896 | tf_op jit(solution)/shard_map/ppermute | solution.py:631
  48.3 3.2 %collective-permute-done.11.two_ref = bf16[216,128]{1,0:T(8,128)(2,1)S(1)} collective-permute-done((bf16[216,128]{1,0:T(8,128)(2,1)S(1)}, bf16[216,128]{1,0:T(8,128)(2,1)S(1)}, u32[]{:S(2)}, u32[]{:S(2)}) %collective-permute-start.11) | collective-permute-done | bytes 55328 | tf_op jit(solution)/shard_map/ppermute | solution.py:631
  51.5 0.0 collective-permute-done.13.two_ref
  51.5 1.3 %collective-permute-start.16 = (bf16[440,128]{1,0:T(8,128)(2,1)S(1)}, bf16[440,128]{1,0:T(8,128)(2,1)S(1)}, u32[]{:S(2)}, u32[]{:S(2)}) collective-permute-start(bf16[440,128]{1,0:T(8,128)(2,1)S(1)} %deep_join.1.refs_0_), channel_id=1, source_target_pairs={{0,6},{1,7},{2,4},{3,5},{4,2},{5,3},{6,0},{7,1},{8,14},{9,15},{10,... | collective-permute-start | bytes 337928 | tf_op jit(solution)/shard_map/ppermute | solution.py:631
  52.8 1.5 %collective-permute-start.15 = (bf16[440,128]{1,0:T(8,128)(2,1)S(1)}, bf16[440,128]{1,0:T(8,128)(2,1)S(1)}, u32[]{:S(2)}, u32[]{:S(2)}) collective-permute-start(bf16[440,128]{1,0:T(8,128)(2,1)S(1)} %deep_join.1.refs_0_), channel_id=1, source_target_pairs={{0,2},{1,3},{2,0},{3,1},{4,6},{5,7},{6,4},{7,5},{8,10},{9,11},{10,... | collective-permute-start | bytes 337928 | tf_op jit(solution)/shard_map/ppermute | solution.py:631
  54.3 0.8 %collective-permute-start.14 = (bf16[440,128]{1,0:T(8,128)(2,1)S(1)}, bf16[440,128]{1,0:T(8,128)(2,1)S(1)}, u32[]{:S(2)}, u32[]{:S(2)}) collective-permute-start(bf16[440,128]{1,0:T(8,128)(2,1)S(1)} %deep_join.1.refs_0_), channel_id=1, source_target_pairs={{0,4},{1,5},{2,6},{3,7},{4,0},{5,1},{6,2},{7,3},{8,12},{9,13},{10,... | collective-permute-start | bytes 337928 | tf_op jit(solution)/shard_map/ppermute | solution.py:631
  55.1 2.3 %collective-permute-done.16.refs_3_ = bf16[440,128]{1,0:T(8,128)(2,1)S(1)} collective-permute-done((bf16[440,128]{1,0:T(8,128)(2,1)S(1)}, bf16[440,128]{1,0:T(8,128)(2,1)S(1)}, u32[]{:S(2)}, u32[]{:S(2)}) %collective-permute-start.16) | collective-permute-done | bytes 112672 | tf_op jit(solution)/shard_map/ppermute | solution.py:631
  57.3 1.1 %collective-permute-done.15.refs_2_ = bf16[440,128]{1,0:T(8,128)(2,1)S(1)} collective-permute-done((bf16[440,128]{1,0:T(8,128)(2,1)S(1)}, bf16[440,128]{1,0:T(8,128)(2,1)S(1)}, u32[]{:S(2)}, u32[]{:S(2)}) %collective-permute-start.15) | collective-permute-done | bytes 112672 | tf_op jit(solution)/shard_map/ppermute | solution.py:631
  58.5 0.6 %collective-permute-done.14.refs_1_ = bf16[440,128]{1,0:T(8,128)(2,1)S(1)} collective-permute-done((bf16[440,128]{1,0:T(8,128)(2,1)S(1)}, bf16[440,128]{1,0:T(8,128)(2,1)S(1)}, u32[]{:S(2)}, u32[]{:S(2)}) %collective-permute-start.14) | collective-permute-done | bytes 112672 | tf_op jit(solution)/shard_map/ppermute | solution.py:631
  59.1 0.1 join.1.chunks_ref
  59.2 0.1 collective-permute-start.17
  59.3 1.0 %finish_own.1 = (f32[192,576]{1,0:T(8,128)}, f32[192,192]{1,0:T(8,128)}, f32[192,768]{1,0:T(8,128)}, f32[192,768]{1,0:T(8,128)}, f32[1,192]{1,0:T(1,128)S(1)}) custom-call(bf16[1760,128]{1,0:T(8,128)(2,1)S(1)} %join.1.chunks_ref), custom_call_target="tpu_custom_call" | custom-call | flops 1000000 | bytes 2097152 | tf_op jit(solution)/shard_map/finish_own/pallas_call | solution.py:572
  60.3 0.7 %collective-permute-done.17.chunks_ref = bf16[1760,128]{1,0:T(8,128)(2,1)S(1)} collective-permute-done((bf16[1760,128]{1,0:T(8,128)(2,1)S(1)}, bf16[1760,128]{1,0:T(8,128)(2,1)S(1)}, u32[]{:S(2)}, u32[]{:S(2)}) %collective-permute-start.17) | collective-permute-done | bytes 450592 | tf_op jit(solution)/shard_map/ppermute | solution.py:631
  61.0 1.0 %finish_far.1 = (f32[192,576]{1,0:T(8,128)}, f32[192,192]{1,0:T(8,128)}, f32[192,768]{1,0:T(8,128)}, f32[192,768]{1,0:T(8,128)}, f32[1,192]{1,0:T(1,128)}) custom-call(bf16[1760,128]{1,0:T(8,128)(2,1)S(1)} %collective-permute-done.17.chunks_ref, ...), custom_call_target="tpu_custom_call", output_to_operand_aliasing={{0}: (2, {}), {1}: (3, {}), {2}: (4, {}), {3}: (5, {})} | custom-call | flops 1000000 | bytes 2097152 | tf_op jit(solution)/shard_map/finish_far/pallas_call | solution.py:572
  (5 shorter events, 0.1 us)
Async XLA Ops:
  3.2 10.6 %collective-permute-start = (bf16[216,384]{1,0:T(8,128)(2,1)}, bf16[216,384]{1,0:T(8,128)(2,1)S(1)}, u32[]{:S(2)}, u32[]{:S(2)}) collective-permute-start(bf16[216,384]{1,0:T(8,128)(2,1)} %get-tuple-element.35), channel_id=1, source_target_pairs={{0,1},{1,2},{2,3},{3,0},{4,5},{5,6},{6,7},{7,4},{8,9},{9,10},{10,1... | collective-permute-start | bytes 497672 | tf_op jit(solution)/shard_map/ppermute | solution.py:631
  3.7 7.9 %collective-permute-start.1 = (bf16[72,384]{1,0:T(8,128)(2,1)}, bf16[72,384]{1,0:T(8,128)(2,1)S(1)}, u32[]{:S(2)}, u32[]{:S(2)}) collective-permute-start(bf16[72,384]{1,0:T(8,128)(2,1)} %get-tuple-element.36), channel_id=1, source_target_pairs={{0,4},{1,5},{2,6},{3,7},{4,8},{5,9},{6,10},{7,11},{8,12},{9,13},{1... | collective-permute-start | bytes 165896 | tf_op jit(solution)/shard_map/ppermute | solution.py:631
  6.3 7.5 %collective-permute-start.2 = (bf16[72,384]{1,0:T(8,128)(2,1)}, bf16[72,384]{1,0:T(8,128)(2,1)S(1)}, u32[]{:S(2)}, u32[]{:S(2)}) collective-permute-start(bf16[72,384]{1,0:T(8,128)(2,1)} %get-tuple-element.37), channel_id=1, source_target_pairs={{0,5},{1,6},{2,7},{3,4},{4,9},{5,10},{6,11},{7,8},{8,13},{9,14},{1... | collective-permute-start | bytes 165896 | tf_op jit(solution)/shard_map/ppermute | solution.py:631
  8.7 1.0 %copy-start.2 = (f32[1,2,6,144,23]{3,1,4,2,0:T(2,128)S(1)}, f32[1,2,6,144,23]{3,1,4,2,0:T(2,128)}, u32[]{:S(2)}) copy-start(f32[1,2,6,144,23]{3,1,4,2,0:T(2,128)} %param.19) | copy-start | bytes 476932
  9.7 4.1 %copy-start = (bf16[192,768]{1,0:T(8,128)(2,1)S(1)}, bf16[192,768]{1,0:T(8,128)(2,1)}, u32[]{:S(2)}) copy-start(bf16[192,768]{1,0:T(8,128)(2,1)} %refs_7_.1) | copy-start | bytes 884740
  9.7 4.1 %copy-start.1 = (bf16[768,192]{0,1:T(8,128)(2,1)S(1)}, bf16[768,192]{0,1:T(8,128)(2,1)}, u32[]{:S(2)}) copy-start(bf16[768,192]{0,1:T(8,128)(2,1)} %param.18) | copy-start | bytes 884740
  9.7 4.1 %copy-start.3 = (bf16[192,576]{1,0:T(8,128)(2,1)S(1)}, bf16[192,576]{1,0:T(8,128)(2,1)}, u32[]{:S(2)}) copy-start(bf16[192,576]{1,0:T(8,128)(2,1)} %refs_5_.1) | copy-start | bytes 663556
  9.7 4.2 %copy-start.4 = (bf16[192,192]{1,0:T(8,128)(2,1)S(1)}, bf16[192,192]{1,0:T(8,128)(2,1)}, u32[]{:S(2)}) copy-start(bf16[192,192]{1,0:T(8,128)(2,1)} %refs_6_.1) | copy-start | bytes 221188
  9.7 4.2 %copy-start.7 = (bf16[216,384]{1,0:T(8,128)(2,1)S(1)}, bf16[216,384]{1,0:T(8,128)(2,1)}, u32[]{:S(2)}) copy-start(bf16[216,384]{1,0:T(8,128)(2,1)} %get-tuple-element.34.refs_0_) | copy-start | bytes 497668
  13.9 19.0 %copy-start.5 = (s32[6,24]{1,0:T(8,128)S(1)}, s32[6,24]{1,0:T(8,128)}, u32[]{:S(2)}) copy-start(s32[6,24]{1,0:T(8,128)} %land_ref.1) | copy-start | bytes 1732
  13.9 19.0 %copy-start.6 = (s32[1,576]{1,0:T(1,128)S(1)}, s32[1,576]{1,0:T(1,128)}, u32[]{:S(2)}) copy-start(s32[1,576]{1,0:T(1,128)} %constant.5.clone.perm_ref) | copy-start | bytes 6916
  22.5 6.8 %collective-permute-start.6 = (bf16[288,768]{1,0:T(8,128)(2,1)S(1)}, bf16[288,768]{1,0:T(8,128)(2,1)S(1)}, u32[]{:S(2)}, u32[]{:S(2)}) collective-permute-start(bf16[288,768]{1,0:T(8,128)(2,1)S(1)} %get-tuple-element.44), channel_id=1, source_target_pairs={{0,1},{1,0},{2,3},{3,2},{4,5},{5,4},{6,7},{7,6},{8,9},{9,8},{10,11... | collective-permute-start | bytes 1327112 | tf_op jit(solution)/shard_map/ppermute | solution.py:631
  22.9 6.4 %collective-permute-start.3 = (bf16[112,384]{1,0:T(8,128)(2,1)S(1)}, bf16[112,384]{1,0:T(8,128)(2,1)S(1)}, u32[]{:S(2)}, u32[]{:S(2)}) collective-permute-start(bf16[112,384]{1,0:T(8,128)(2,1)S(1)} %get-tuple-element.39), channel_id=1, source_target_pairs={{0,3},{1,0},{2,1},{3,2},{4,7},{5,4},{6,5},{7,6},{8,11},{9,8},{10,9... | collective-permute-start | bytes 258056 | tf_op jit(solution)/shard_map/ppermute | solution.py:631
  24.2 3.9 %collective-permute-start.4 = (bf16[40,384]{1,0:T(8,128)(2,1)S(1)}, bf16[40,384]{1,0:T(8,128)(2,1)S(1)}, u32[]{:S(2)}, u32[]{:S(2)}) collective-permute-start(bf16[40,384]{1,0:T(8,128)(2,1)S(1)} %get-tuple-element.40), channel_id=1, source_target_pairs={{0,28},{1,29},{2,30},{3,31},{4,0},{5,1},{6,2},{7,3},{8,4},{9,5},{1... | collective-permute-start | bytes 92168 | tf_op jit(solution)/shard_map/ppermute | solution.py:631
  25.8 3.4 %collective-permute-start.5 = (bf16[40,384]{1,0:T(8,128)(2,1)S(1)}, bf16[40,384]{1,0:T(8,128)(2,1)S(1)}, u32[]{:S(2)}, u32[]{:S(2)}) collective-permute-start(bf16[40,384]{1,0:T(8,128)(2,1)S(1)} %get-tuple-element.41), channel_id=1, source_target_pairs={{0,31},{1,28},{2,29},{3,30},{4,3},{5,0},{6,1},{7,2},{8,7},{9,4},{1... | collective-permute-start | bytes 92168 | tf_op jit(solution)/shard_map/ppermute | solution.py:631
  29.3 4.8 %collective-permute-start.7 = (bf16[72,768]{1,0:T(8,128)(2,1)S(1)}, bf16[72,768]{1,0:T(8,128)(2,1)S(1)}, u32[]{:S(2)}, u32[]{:S(2)}) collective-permute-start(bf16[72,768]{1,0:T(8,128)(2,1)S(1)} %get-tuple-element.46), channel_id=1, source_target_pairs={{0,4},{1,5},{2,6},{3,7},{4,0},{5,1},{6,2},{7,3},{8,12},{9,13},{10,... | collective-permute-start | bytes 331784 | tf_op jit(solution)/shard_map/ppermute | solution.py:631
  30.7 7.1 %collective-permute-start.8 = (bf16[72,768]{1,0:T(8,128)(2,1)S(1)}, bf16[72,768]{1,0:T(8,128)(2,1)S(1)}, u32[]{:S(2)}, u32[]{:S(2)}) collective-permute-start(bf16[72,768]{1,0:T(8,128)(2,1)S(1)} %get-tuple-element.47), channel_id=1, source_target_pairs={{0,2},{1,3},{2,0},{3,1},{4,6},{5,7},{6,4},{7,5},{8,10},{9,11},{10,... | collective-permute-start | bytes 331784 | tf_op jit(solution)/shard_map/ppermute | solution.py:631
  31.3 6.5 %collective-permute-start.9 = (bf16[72,768]{1,0:T(8,128)(2,1)S(1)}, bf16[72,768]{1,0:T(8,128)(2,1)S(1)}, u32[]{:S(2)}, u32[]{:S(2)}) collective-permute-start(bf16[72,768]{1,0:T(8,128)(2,1)S(1)} %get-tuple-element.48), channel_id=1, source_target_pairs={{0,6},{1,7},{2,4},{3,5},{4,2},{5,3},{6,0},{7,1},{8,14},{9,15},{10,... | collective-permute-start | bytes 331784 | tf_op jit(solution)/shard_map/ppermute | solution.py:631
  37.9 6.0 %collective-permute-start.12 = (bf16[224,128]{1,0:T(8,128)(2,1)S(1)}, bf16[224,128]{1,0:T(8,128)(2,1)S(1)}, u32[]{:S(2)}, u32[]{:S(2)}) collective-permute-start(bf16[224,128]{1,0:T(8,128)(2,1)S(1)} %get-tuple-element.51.one_ref), channel_id=1, source_target_pairs={{0,24},{1,25},{2,26},{3,27},{4,28},{5,29},{6,30},{7,31},{8,16},{9,... | collective-permute-start | bytes 172040 | tf_op jit(solution)/shard_map/ppermute | solution.py:631
  41.5 4.2 %collective-permute-start.10 = (bf16[216,128]{1,0:T(8,128)(2,1)S(1)}, bf16[216,128]{1,0:T(8,128)(2,1)S(1)}, u32[]{:S(2)}, u32[]{:S(2)}) collective-permute-start(bf16[216,128]{1,0:T(8,128)(2,1)S(1)} %get-tuple-element.50.one_ref), channel_id=1, source_target_pairs={{0,8},{1,9},{2,10},{3,11},{4,12},{5,13},{6,14},{7,15},{8,0},{9,1},... | collective-permute-start | bytes 165896 | tf_op jit(solution)/shard_map/ppermute | solution.py:631
  43.9 7.5 %collective-permute-start.13 = (bf16[224,128]{1,0:T(8,128)(2,1)S(1)}, bf16[224,128]{1,0:T(8,128)(2,1)S(1)}, u32[]{:S(2)}, u32[]{:S(2)}) collective-permute-start(bf16[224,128]{1,0:T(8,128)(2,1)S(1)} %deep_add.6.one_ref), channel_id=1, source_target_pairs={{0,8},{1,9},{2,10},{3,11},{4,12},{5,13},{6,14},{7,15},{8,0},{9,1},... | collective-permute-start | bytes 172040 | tf_op jit(solution)/shard_map/ppermute | solution.py:631
  45.7 5.7 %collective-permute-start.11 = (bf16[216,128]{1,0:T(8,128)(2,1)S(1)}, bf16[216,128]{1,0:T(8,128)(2,1)S(1)}, u32[]{:S(2)}, u32[]{:S(2)}) collective-permute-start(bf16[216,128]{1,0:T(8,128)(2,1)S(1)} %deep_add.4.one_ref), channel_id=1, source_target_pairs={{0,16},{1,17},{2,18},{3,19},{4,20},{5,21},{6,22},{7,23},{8,24},{9,... | collective-permute-start | bytes 165896 | tf_op jit(solution)/shard_map/ppermute | solution.py:631
  51.5 5.8 %collective-permute-start.16 = (bf16[440,128]{1,0:T(8,128)(2,1)S(1)}, bf16[440,128]{1,0:T(8,128)(2,1)S(1)}, u32[]{:S(2)}, u32[]{:S(2)}) collective-permute-start(bf16[440,128]{1,0:T(8,128)(2,1)S(1)} %deep_join.1.refs_0_), channel_id=1, source_target_pairs={{0,6},{1,7},{2,4},{3,5},{4,2},{5,3},{6,0},{7,1},{8,14},{9,15},{10,... | collective-permute-start | bytes 337928 | tf_op jit(solution)/shard_map/ppermute | solution.py:631
  52.8 5.7 %collective-permute-start.15 = (bf16[440,128]{1,0:T(8,128)(2,1)S(1)}, bf16[440,128]{1,0:T(8,128)(2,1)S(1)}, u32[]{:S(2)}, u32[]{:S(2)}) collective-permute-start(bf16[440,128]{1,0:T(8,128)(2,1)S(1)} %deep_join.1.refs_0_), channel_id=1, source_target_pairs={{0,2},{1,3},{2,0},{3,1},{4,6},{5,7},{6,4},{7,5},{8,10},{9,11},{10,... | collective-permute-start | bytes 337928 | tf_op jit(solution)/shard_map/ppermute | solution.py:631
  54.3 4.8 %collective-permute-start.14 = (bf16[440,128]{1,0:T(8,128)(2,1)S(1)}, bf16[440,128]{1,0:T(8,128)(2,1)S(1)}, u32[]{:S(2)}, u32[]{:S(2)}) collective-permute-start(bf16[440,128]{1,0:T(8,128)(2,1)S(1)} %deep_join.1.refs_0_), channel_id=1, source_target_pairs={{0,4},{1,5},{2,6},{3,7},{4,0},{5,1},{6,2},{7,3},{8,12},{9,13},{10,... | collective-permute-start | bytes 337928 | tf_op jit(solution)/shard_map/ppermute | solution.py:631
  59.2 1.9 %collective-permute-start.17 = (bf16[1760,128]{1,0:T(8,128)(2,1)S(1)}, bf16[1760,128]{1,0:T(8,128)(2,1)S(1)}, u32[]{:S(2)}, u32[]{:S(2)}) collective-permute-start(bf16[1760,128]{1,0:T(8,128)(2,1)S(1)} %join.1.chunks_ref), channel_id=1, source_target_pairs={{0,1},{1,0},{2,3},{3,2},{4,5},{5,4},{6,7},{7,6},{8,9},{9,8},{10,11... | collective-permute-start | bytes 1351688 | tf_op jit(solution)/shard_map/ppermute | solution.py:631
where the time goes:
time: 62.3 us; the launch traced here: 62.1 us
  starting transfers between devices  23.1 us (37%)
  waiting for transfers between devices  21 us (34%)
  Pallas kernels  16.2 us (26%)
  local copies, waits for them, and re-layouts  0.99 us (2%)
  between operations  0.8 us (1%)
    ppermute x18, starting transfers between devices, send(): return lax.ppermute(value, AXES, pairs)  23.1 us
    ppermute x18, waiting for transfers between devices, send(): return lax.ppermute(value, AXES, pairs)  21 us
    pallas_call x1, Pallas kernels, block(): pl.pallas_call(functools.partial(block_kernel, windows, lon_windows, size...  8.58 us
    pallas_call x1, Pallas kernels, pack(): pl.pallas_call(functools.partial(pack_kernel, rows, cols), out_shape=[sha...  2.58 us
    pallas_call x2, Pallas kernels, finish(): pl.pallas_call(functools.partial(finish_kernel, bool(before)), out_shape=...  2.08 us
    pallas_call x1, Pallas kernels, expand_bias(): pl.pallas_call(functools.partial(bias_kernel, levels), out_shape=shape((g...  1.42 us
  transfers between devices with their start and end apart: 18, of which 13 were waited for; matrix products, arithmetic and copies ran while one was open for 0% of the time, Pallas kernels for 6%

commit v1 on v0

--- a/solution.py
+++ b/solution.py
@@ -42,7 +42,6 @@
 BLOCKS = FF // 128
 EXTRA = 8
 FULL = BLOCKS * CHUNK + EXTRA
-FIRST = FULL // 16 * 8
 
 
 def mm(a, b):
@@ -294,17 +293,11 @@
         out[...] = jnp.concatenate(parts, axis=0).astype(out.dtype)
 
 
-def forward_kernel(
-    windows, lon_windows,
-    own_ref, north_ref, side_ref, corner_ref, bias_ref, triple_ref, project_ref, up_ref, down_ref,
-    q_ref, k_ref, v_ref, p_ref, mixed_ref, normed_ref, unit_ref, spread_ref, gsum_ref, up_grad_ref, down_grad_ref,
-    branch_ref, cot_ref, emb_ref,
-):
-    pieces = [ref[...].astype(f32) for ref in (own_ref, north_ref, side_ref, corner_ref)]
-    runs = [run for window in window_runs(lon_windows) for run in window]
+def attend(first, runs, pieces, bias_ref, triple_ref, project_ref, *refs):
+    q_ref, k_ref, v_ref, p_ref, mixed_ref, normed_ref, unit_ref, spread_ref, summed_ref, cot_ref = refs
+    pieces = [piece.astype(f32) for piece in pieces]
     ordered = jnp.concatenate([pieces[n][start : start + count] for n, start, count in runs], axis=0)
     emb = ordered[:, :C]
-    emb_ref[...] = emb
     cot_ref[...] = ordered[:, C:].astype(bf16)
     unit, spread = unit_norm(emb)
     unit_ref[...] = unit
@@ -317,27 +310,24 @@
     v_ref[...] = packed[:, 2 * C :].astype(bf16)
     masks = head_masks(TOK)
     masks_b = [mask.astype(bf16) for mask in masks]
-
-    def window_step(w, carry):
-        rows = pl.ds(pl.multiple_of(w * TOK, TOK), TOK)
-        level = w % (Z // WZ)
+    for w in range(emb.shape[0] // TOK):
+        rows = slice(w * TOK, (w + 1) * TOK)
+        heads = slice(w * HEADS, (w + 1) * HEADS)
+        level = (first + w) % (Z // WZ)
         scores = mm_nt(stacked(q_ref[rows, :], masks_b), k_ref[rows, :])
-        bias = bias_ref[pl.ds(level * HEADS, HEADS)].reshape(HEADS * TOK, TOK)
+        bias = bias_ref[level * HEADS : (level + 1) * HEADS].reshape(HEADS * TOK, TOK)
         raised = jnp.exp2(scores * (score_scale * log2e) + bias)
         probs = raised * (1.0 / jnp.sum(raised, -1, keepdims=True))
         probs_b = probs.astype(bf16)
-        p_ref[pl.ds(w * HEADS, HEADS)] = probs_b.reshape(HEADS, TOK, TOK)
+        p_ref[heads] = probs_b.reshape(HEADS, TOK, TOK)
         mixed = head_sum(mm(probs_b, v_ref[rows, :]), masks).astype(bf16)
         mixed_ref[rows, :] = mixed
-        branch_ref[rows, :] = mm(mixed, project_ref[...])
-        return carry
-
-    lax.fori_loop(0, windows, window_step, 0, unroll=True)
-
-    attended = branch_ref[...].astype(bf16).astype(f32)
-    unit2, spread2 = unit_norm(emb_ref[...] + attended)
+        summed_ref[rows, :] = emb[rows] + mm(mixed, project_ref[...]).astype(bf16).astype(f32)
+
+
+def feed_back(summed, cot, up_ref, down_ref, gsum_ref, up_grad_ref, down_grad_ref):
+    unit2, spread2 = unit_norm(summed)
     normed2 = unit2.astype(bf16)
-    cot = cot_ref[...]
     back = jnp.zeros(unit2.shape, f32)
     block = 256
     for start in range(0, FF, block):
@@ -355,16 +345,15 @@
     gsum_ref[...] = cot.astype(f32) + norm_back(back, unit2, spread2)
 
 
-def windows_back_kernel(windows, q_ref, k_ref, v_ref, p_ref, gsum_ref, project_ref, gq_ref, gk_ref, gv_ref):
+def attend_back(at, q_ref, k_ref, v_ref, p_ref, gsum_ref, project_ref, gq_ref, gk_ref, gv_ref):
     masks = head_masks(TOK)
     masks_b = [mask.astype(bf16) for mask in masks]
-
-    def window_step(w, carry):
-        rows = pl.ds(pl.multiple_of(w * TOK, TOK), TOK)
-        grad = gsum_ref[rows, :].astype(bf16)
-        grad_mixed = mm_nt(grad, project_ref[...])
-        grad_mixed_b = grad_mixed.astype(bf16)
-        probs_b = p_ref[pl.ds(w * HEADS, HEADS)].reshape(HEADS * TOK, TOK)
+    for w in range(q_ref.shape[0] // TOK):
+        rows = slice(w * TOK, (w + 1) * TOK)
+        full_rows = slice(at + w * TOK, at + (w + 1) * TOK)
+        grad = gsum_ref[full_rows, :].astype(bf16)
+        grad_mixed_b = mm_nt(grad, project_ref[...]).astype(bf16)
+        probs_b = p_ref[w * HEADS : (w + 1) * HEADS].reshape(HEADS * TOK, TOK)
         probs = probs_b.astype(f32)
         grad_probs = mm_nt(stacked(grad_mixed_b, masks_b), v_ref[rows, :])
         inner = jnp.sum(grad_probs * probs, -1, keepdims=True)
@@ -378,35 +367,31 @@
             span = slice(h * TOK, (h + 1) * TOK)
             grad_k.append(mm(query_t[spot], scaled[span]))
             grad_v.append(mm(grad_mixed_t[spot], probs_b[span]))
-        gq_ref[rows, :] = grad_q.astype(bf16)
-        gk_ref[rows, :] = jnp.concatenate(grad_k, axis=0).T.astype(bf16)
-        gv_ref[rows, :] = jnp.concatenate(grad_v, axis=0).T.astype(bf16)
-        return carry
-
-    lax.fori_loop(0, windows, window_step, 0, unroll=True)
+        gq_ref[full_rows, :] = grad_q.astype(bf16)
+        gk_ref[full_rows, :] = jnp.concatenate(grad_k, axis=0).T.astype(bf16)
+        gv_ref[full_rows, :] = jnp.concatenate(grad_v, axis=0).T.astype(bf16)
 
 
 def halved(rows):
     return -(-rows // 16) * 8
 
 
-def tokens_back_kernel(
-    lon_windows, sizes, gq_ref, gk_ref, gv_ref, mixed_ref, normed_ref, unit_ref, spread_ref, gsum_ref, triple_ref,
-    up_grad_ref, down_grad_ref, *rest,
+def tokens_back(
+    lon_windows, sizes, gq_ref, gk_ref, gv_ref, mixed, normed, unit, spread, gsum_ref, triple_ref, up_grad_ref, down_grad_ref,
+    *rest,
 ):
     outs, (keep_ref, send_ref, total_ref) = rest[: len(sizes)], rest[len(sizes) :]
-    normed = normed_ref[...]
     triple = triple_ref[...]
-    grad_normed = jnp.zeros(unit_ref.shape, f32)
+    grad_normed = jnp.zeros(unit.shape, f32)
     parts = []
     for n, ref in enumerate((gq_ref, gk_ref, gv_ref)):
         grad = ref[...]
         grad_normed = grad_normed + mm_nt(grad, triple[:, n * C : (n + 1) * C])
         parts.append(mm_tn(normed, grad))
-    parts.append(mm_tn(mixed_ref[...], gsum_ref[...].astype(bf16)))
+    parts.append(mm_tn(mixed, gsum_ref[...].astype(bf16)))
     total_ref[...] = jnp.concatenate(parts, axis=1)
     grad_normed = grad_normed.astype(bf16).astype(f32)
-    grad_tokens = gsum_ref[...] + norm_back(grad_normed, unit_ref[...], spread_ref[...])
+    grad_tokens = gsum_ref[...] + norm_back(grad_normed, unit, spread)
     parts, at = [[] for _ in sizes], 0
     for n, start, count in [run for window in window_runs(lon_windows) for run in window]:
         parts[n].append((start, grad_tokens[at : at + count]))
@@ -419,46 +404,75 @@
     split_parts((up_grad_ref, down_grad_ref, total_ref), keep_ref, send_ref)
 
 
-def block_kernel(windows, lon_windows, sizes, *refs):
-    ins, refs = refs[:9], refs[9:]
-    pieces, (bias_ref, triple_ref, project_ref, up_ref, down_ref) = ins[:4], ins[4:]
+def saved_shapes(count):
+    dims = [((count, C), bf16)] * 3 + [((count // TOK * HEADS, TOK, TOK), bf16)] + [((count, C), bf16)] * 2
+    return dims + [((count, C), f32), ((count, 1), f32), ((count, C), f32), ((count, C), bf16)]
+
+
+SAVED = len(saved_shapes(TOK))
+
+
+def split_runs(lon_windows):
+    windows = window_runs(lon_windows)
+    whole = (lon_windows - 1) * (Z // WZ)
+    return whole, *[[run for window in part for run in window] for part in (windows[:whole], windows[whole:])]
+
+
+def near_kernel(lon_windows, own_ref, north_ref, *refs):
+    runs = split_runs(lon_windows)[1]
+    attend(0, runs, (own_ref[...], north_ref[...]), *refs)
+
+
+def near_block(own, north, bias, triple, project, lon_windows):
+    count = split_runs(lon_windows)[0] * TOK
+    return pl.pallas_call(
+        functools.partial(near_kernel, lon_windows),
+        out_shape=[shape(*dims) for dims in saved_shapes(count)],
+        in_specs=vmem(5),
+        out_specs=vmem(SAVED),
+        compiler_params=pltpu.CompilerParams(vmem_limit_bytes=24 * MIB),
+        cost_estimate=cost(3 * 10**9, 8 * MIB),
+        name="near_block",
+    )(own, north, bias, triple, project)
+
+
+def block_kernel(lon_windows, sizes, *refs):
+    whole, _, runs = split_runs(lon_windows)
+    pieces, refs = refs[:4], refs[4:]
+    (bias_ref, triple_ref, project_ref, up_ref, down_ref), refs = refs[:5], refs[5:]
+    near, refs = refs[:SAVED], refs[SAVED:]
     outs, refs = refs[: len(sizes) + 2], refs[len(sizes) + 2 :]
-    q, k, v, p, mixed, normed, unit, spread, gsum, up_grad, down_grad, branch, cot, emb, gq, gk, gv, total = refs
-    forward_kernel(
-        windows, lon_windows, *pieces, bias_ref, triple_ref, project_ref, up_ref, down_ref,
-        q, k, v, p, mixed, normed, unit, spread, gsum, up_grad, down_grad, branch, cot, emb,
-    )
-    windows_back_kernel(windows, q, k, v, p, gsum, project_ref, gq, gk, gv)
-    tokens_back_kernel(
-        lon_windows, sizes, gq, gk, gv, mixed, normed, unit, spread, gsum, triple_ref, up_grad, down_grad, *outs, total
-    )
-
-
-def block(pieces, bias, triple, project, up, down, lon_windows, sizes):
+    far, (gsum, up_grad, down_grad, gq, gk, gv, total) = refs[:SAVED], refs[SAVED:]
+    attend(whole, runs, [ref[...] for ref in pieces], bias_ref, triple_ref, project_ref, *far)
+    mixed, normed, unit, spread, summed, cot = [
+        jnp.concatenate([one[...], other[...]], axis=0) for one, other in zip(near[4:], far[4:])
+    ]
+    feed_back(summed, cot, up_ref, down_ref, gsum, up_grad, down_grad)
+    attend_back(0, *near[:4], gsum, project_ref, gq, gk, gv)
+    attend_back(whole * TOK, *far[:4], gsum, project_ref, gq, gk, gv)
+    tokens_back(lon_windows, sizes, gq, gk, gv, mixed, normed, unit, spread, gsum, triple_ref, up_grad, down_grad, *outs, total)
+
+
+def block(pieces, bias, triple, project, up, down, near, lon_windows, sizes):
     count = sum(sizes)
-    windows = count // TOK
     out_shape = [shape((halved(size), 2 * C), bf16) for size in sizes] + [
         shape((QUADS * CHUNK, FF), f32),
         shape((QUADS * CHUNK, FF), bf16),
     ]
-    rows = [pltpu.VMEM((count, C), dtype) for dtype in (bf16, f32)]
     return pl.pallas_call(
-        functools.partial(block_kernel, windows, lon_windows, sizes),
+        functools.partial(block_kernel, lon_windows, sizes),
         out_shape=out_shape,
-        in_specs=vmem(9),
+        in_specs=vmem(9 + SAVED),
         out_specs=vmem(len(out_shape)),
-        scratch_shapes=rows[:1] * 3
-        + [pltpu.VMEM((windows * HEADS, TOK, TOK), bf16)]
-        + rows[:1] * 2
-        + [rows[1], pltpu.VMEM((count, 1), f32), rows[1]]
+        scratch_shapes=[pltpu.VMEM(*dims) for dims in saved_shapes(count - near[0].shape[0])]
+        + [pltpu.VMEM((count, C), f32)]
         + [pltpu.VMEM((C, FF), f32)] * 2
-        + [rows[1], rows[0], rows[1]]
-        + rows[:1] * 3
+        + [pltpu.VMEM((count, C), bf16)] * 3
         + [pltpu.VMEM((C, FF), f32)],
-        compiler_params=pltpu.CompilerParams(vmem_limit_bytes=32 * MIB),
+        compiler_params=pltpu.CompilerParams(vmem_limit_bytes=28 * MIB),
         cost_estimate=cost(8 * 10**9, 16 * MIB),
         name="block",
-    )(*pieces, bias, triple, project, up, down)
+    )(*pieces, bias, triple, project, up, down, *near)
 
 
 def home_kernel(sizes, rows, cols, own_ref, north_ref, side_ref, corner_ref, perm_ref, land_ref, out_ref, sum_ref):
@@ -496,7 +510,7 @@
 
 
 def chip_add_kernel(keep_ref, *refs):
-    gots, (land_ref, first_ref, second_ref) = refs[:-3], refs[-3:]
+    gots, (land_ref, out_ref) = refs[:-2], refs[-2:]
     total = keep_ref[...]
     for ref in gots:
         total = total + ref[...].astype(f32)
@@ -504,8 +518,7 @@
     rest = jnp.concatenate([land[:, 128:], jnp.zeros((1, 2 * 128 - C), f32)], axis=1)
     parts = [total[:, n * 128 : (n + 1) * 128] for n in range(BLOCKS)]
     total = jnp.concatenate(parts + [land[:, :128], rest, jnp.zeros((EXTRA - 2, 128), f32)], axis=0)
-    first_ref[...] = total[:FIRST].astype(bf16)
-    second_ref[...] = total[FIRST:].astype(bf16)
+    out_ref[...] = total.astype(bf16)
 
 
 def add_kernel(one_ref, two_ref, out_ref):
@@ -602,17 +615,13 @@
     parts = [shape((CHUNK, FF), f32)] + one(CHUNK) * (QUADS - 1)
     own, *parts = small_call(core_add_kernel, parts, (keep, got), "core_add", after=after)
     gots = [shift(value, move=chip_move(e)) for e, value in enumerate(parts, 1)]
-    sides = [shape((rows, 128), bf16) for rows in (FIRST, FULL - FIRST)]
-    totals = small_call(chip_add_kernel, sides, (own, *gots, land), "chip_add")
-    steps = [(1, 3), (2, 1)]
-    while 2 ** len(steps) < lon_count // 2:
-        steps.append((2 ** len(steps),) * 2)
-    for step in steps:
-        gots = [shift(total, move=deep_move(e)) for total, e in zip(totals, step)]
-        totals = [
-            small_call(add_kernel, [side], pair, "deep_add")[0] for side, pair in zip(sides, zip(totals, gots))
-        ]
-    (total,) = small_call(join_kernel, [shape((FULL, 128), bf16)], totals, "deep_join")
+    full = [shape((FULL, 128), bf16)]
+    (total,) = small_call(chip_add_kernel, full, (own, *gots, land), "chip_add")
+    reach = 1
+    while reach < lon_count // 2:
+        got = shift(total, move=deep_move(reach))
+        reach *= 2
+        (total,) = small_call(add_kernel, full, (total, got), "deep_add")
     near = [total] + [shift(total, move=chip_move(e)) for e in range(1, QUADS)]
     (total,) = small_call(join_kernel, [shape((QUADS * FULL, 128), bf16)], near, "join")
     got = shift(total, move=core_move)
@@ -647,8 +656,9 @@
 
     sizes = [part.size for part in piece_rows(rows, cols)]
     pieces = (own, north, side, corner)
+    near = near_block(own, north, bias, triple_weight, project_weight, lon_windows)
     own, north, side, corner, keep, sent = block(
-        pieces, bias, triple_weight, project_weight, up_weight, down_weight.T, lon_windows, sizes
+        pieces, bias, triple_weight, project_weight, up_weight, down_weight.T, near, lon_windows, sizes
     )
     north = shift(north, move=lambda lon, lat: (lon, lat - 1))
     side = shift(side, move=lambda lon, lat: (lon - 1, lat))

time: 62.3 us -> 59.8 us (0.960)
  starting transfers between devices: 23.1 us -> 20.1 us
    ppermute x18 -> x16, starting transfers between devices: 23.1 us -> 20.1 us  [send(): return lax.ppermute(value, AXES, pairs)]
    pallas_call x1 -> x2, Pallas kernels: 8.58 us -> 9.25 us  [the longest x1 7.47 us: block(): pl.pallas_call(functools.partial(block_kernel, lon_windows, sizes), out_s...]
    ppermute x18 -> x16, waiting for transfers between devices: 21 us -> 20.9 us  [send(): return lax.ppermute(value, AXES, pairs)]
  transfers between devices with their start and end apart: 18 -> 16, of which waited for: 13 -> 12; matrix products, arithmetic and copies ran while one was open for 0% -> 0% of each run, Pallas kernels for 6% -> 9%
where the time goes in v1:
time: 59.8 us; the launch traced here: 59.6 us
  waiting for transfers between devices  20.9 us (35%)
  starting transfers between devices  20.1 us (34%)
  Pallas kernels  16.8 us (28%)
  local copies, waits for them, and re-layouts  0.99 us (2%)
  between operations  0.78 us (1%)
    ppermute x16, waiting for transfers between devices, send(): return lax.ppermute(value, AXES, pairs)  20.9 us
    ppermute x16, starting transfers between devices, send(): return lax.ppermute(value, AXES, pairs)  20.1 us
    pallas_call x1, Pallas kernels, block(): pl.pallas_call(functools.partial(block_kernel, lon_windows, sizes), out_s...  7.47 us
    pallas_call x1, Pallas kernels, pack(): pl.pallas_call(functools.partial(pack_kernel, rows, cols), out_shape=[sha...  2.58 us
    pallas_call x2, Pallas kernels, finish(): pl.pallas_call(functools.partial(finish_kernel, bool(before)), out_shape=...  2.08 us
    pallas_call x1, Pallas kernels, near_block(): pl.pallas_call(functools.partial(near_kernel, lon_windows), out_shape=[sh...  1.79 us
    pallas_call x1, Pallas kernels, expand_bias(): pl.pallas_call(functools.partial(bias_kernel, levels), out_shape=shape((g...  1.42 us
    pallas_call x1, Pallas kernels, to_home(): pl.pallas_call(functools.partial(home_kernel, sizes, rows, cols), out_sha...  1.22 us
  transfers between devices with their start and end apart: 16, of which 12 were waited for; matrix products, arithmetic and copies ran while one was open for 0% of the time, Pallas kernels for 9%

profile of v1, /device:TPU:0, one launch (start us, length us, event | category | flops | bytes accessed | tf_op | source)
XLA Modules:
  0.0 59.6 jit_solution(8773869681899974369)
XLA Ops:
  0.6 2.6 %pack.1 = (bf16[216,384]{1,0:T(8,128)(2,1)}, bf16[216,384]{1,0:T(8,128)(2,1)}, bf16[72,384]{1,0:T(8,128)(2,1)}, bf16[72,384]{1,0:T(8,128)(2,1)}) custom-call(bf16[576,192]{1,0:T(8,128)(2,1)} %bitcast.15, bf16[576,192]{1,0:T(8,128)(2,1)} %bitcast.16, s32[6,24]{1,0:T(8,128)} %land_ref.1, f32[1,192]{1,0:T(1,128)} %bitcast.17, s32[1,576]{1,0:T(1,128)} %constant.4.clone.refs_4_), custom_call_target="tpu_custom_call" | custom-call | flops 254803968 | bytes 4194304 | tf_op jit(solution)/shard_map/pack/pallas_call | solution.py:161
  3.2 0.5 collective-permute-start
  3.7 2.6 %collective-permute-start.1 = (bf16[72,384]{1,0:T(8,128)(2,1)}, bf16[72,384]{1,0:T(8,128)(2,1)S(1)}, u32[]{:S(2)}, u32[]{:S(2)}) collective-permute-start(bf16[72,384]{1,0:T(8,128)(2,1)} %get-tuple-element.44), channel_id=1, source_target_pairs={{0,4},{1,5},{2,6},{3,7},{4,8},{5,9},{6,10},{7,11},{8,12},{9,13},{1... | collective-permute-start | bytes 165896 | tf_op jit(solution)/shard_map/ppermute | solution.py:640
  6.3 2.4 %collective-permute-start.2 = (bf16[72,384]{1,0:T(8,128)(2,1)}, bf16[72,384]{1,0:T(8,128)(2,1)S(1)}, u32[]{:S(2)}, u32[]{:S(2)}) collective-permute-start(bf16[72,384]{1,0:T(8,128)(2,1)} %get-tuple-element.45), channel_id=1, source_target_pairs={{0,5},{1,6},{2,7},{3,4},{4,9},{5,10},{6,11},{7,8},{8,13},{9,14},{1... | collective-permute-start | bytes 165896 | tf_op jit(solution)/shard_map/ppermute | solution.py:640
  8.7 0.0 copy-start.2
  8.7 1.0 %copy-done.2 = f32[1,2,6,144,23]{3,1,4,2,0:T(2,128)S(1)} copy-done((f32[1,2,6,144,23]{3,1,4,2,0:T(2,128)S(1)}, f32[1,2,6,144,23]{3,1,4,2,0:T(2,128)}, u32[]{:S(2)}) %copy-start.2) | copy-done | bytes 159000
  9.7 0.0 copy-start.3
  9.7 0.0 copy-start.4
  9.7 0.0 copy-start.7
  9.7 1.4 %bias.1.refs_0_.refs_4_ = f32[12,144,144]{2,1,0:T(8,128)S(1)} custom-call(f32[138,2,144]{2,1,0:T(2,128)S(1)} %bitcast.13), custom_call_target="tpu_custom_call" | custom-call | flops 1000000000 | bytes 8388608 | tf_op jit(solution)/shard_map/bias/pallas_call | solution.py:250
  11.1 0.0 collective-permute-done.north_ref.refs_1_
  11.1 0.0 copy-done.3
  11.1 0.0 copy-done.4
  11.1 0.0 copy-done.7
  11.1 0.0 copy-start
  11.2 0.0 copy-start.1
  11.2 1.8 %near_block.1 = (bf16[288,192]{1,0:T(8,128)(2,1)S(1)}, bf16[288,192]{1,0:T(8,128)(2,1)S(1)}, bf16[288,192]{1,0:T(8,128)(2,1)S(1)}, bf16[12,144,144]{2,1,0:T(8,12...) custom-call(bf16[216,384]{1,0:T(8,128)(2,1)S(1)} %copy-done.7, ...), custom_call_target="tpu_custom_call" | custom-call | flops 3000000000 | bytes 8388608 | tf_op jit(solution)/shard_map/near_block/pallas_call | solution.py:428
  13.0 0.0 collective-permute-done.1.refs_2_
  13.0 0.8 %collective-permute-done.2.refs_3_ = bf16[72,384]{1,0:T(8,128)(2,1)S(1)} collective-permute-done((bf16[72,384]{1,0:T(8,128)(2,1)}, bf16[72,384]{1,0:T(8,128)(2,1)S(1)}, u32[]{:S(2)}, u32[]{:S(2)}) %collective-permute-start.2) | collective-permute-done | bytes 55328 | tf_op jit(solution)/shard_map/ppermute | solution.py:640
  13.8 0.0 copy-done
  13.8 0.0 copy-done.1
  13.8 0.0 copy-start.5
  13.8 0.0 copy-start.6
  13.8 7.5 %block.1 = (bf16[112,384]{1,0:T(8,128)(2,1)S(1)}, bf16[112,384]{1,0:T(8,128)(2,1)S(1)}, bf16[40,384]{1,0:T(8,128)(2,1)S(1)}, bf16[40,384]{1,0:T(8,128)(2,1)S(1)}...) custom-call(bf16[216,384]{1,0:T(8,128)(2,1)S(1)} %copy-done.7, ...), custom_call_target="tpu_custom_call" | custom-call | flops 8000000000 | bytes 16777216 | tf_op jit(solution)/shard_map/block/pallas_call | solution.py:462
  21.3 0.4 collective-permute-start.6
  21.7 1.3 %collective-permute-start.3 = (bf16[112,384]{1,0:T(8,128)(2,1)S(1)}, bf16[112,384]{1,0:T(8,128)(2,1)S(1)}, u32[]{:S(2)}, u32[]{:S(2)}) collective-permute-start(bf16[112,384]{1,0:T(8,128)(2,1)S(1)} %get-tuple-element.57), channel_id=1, source_target_pairs={{0,3},{1,0},{2,1},{3,2},{4,7},{5,4},{6,5},{7,6},{8,11},{9,8},{10,9... | collective-permute-start | bytes 258056 | tf_op jit(solution)/shard_map/ppermute | solution.py:640
  23.0 2.3 %collective-permute-start.4 = (bf16[40,384]{1,0:T(8,128)(2,1)S(1)}, bf16[40,384]{1,0:T(8,128)(2,1)S(1)}, u32[]{:S(2)}, u32[]{:S(2)}) collective-permute-start(bf16[40,384]{1,0:T(8,128)(2,1)S(1)} %get-tuple-element.58), channel_id=1, source_target_pairs={{0,28},{1,29},{2,30},{3,31},{4,0},{5,1},{6,2},{7,3},{8,4},{9,5},{1... | collective-permute-start | bytes 92168 | tf_op jit(solution)/shard_map/ppermute | solution.py:640
  25.3 0.2 collective-permute-start.5
  25.5 1.4 %collective-permute-done.4.side_ref.refs_1_ = bf16[40,384]{1,0:T(8,128)(2,1)S(1)} collective-permute-done((bf16[40,384]{1,0:T(8,128)(2,1)S(1)}, bf16[40,384]{1,0:T(8,128)(2,1)S(1)}, u32[]{:S(2)}, u32[]{:S(2)}) %collective-permute-start.4) | collective-permute-done | bytes 30752 | tf_op jit(solution)/shard_map/ppermute | solution.py:640
  26.9 1.8 %collective-permute-done.5.corner_ref.refs_2_ = bf16[40,384]{1,0:T(8,128)(2,1)S(1)} collective-permute-done((bf16[40,384]{1,0:T(8,128)(2,1)S(1)}, bf16[40,384]{1,0:T(8,128)(2,1)S(1)}, u32[]{:S(2)}, u32[]{:S(2)}) %collective-permute-start.5) | collective-permute-done | bytes 30752 | tf_op jit(solution)/shard_map/ppermute | solution.py:640
  28.7 0.0 collective-permute-done.3.north_ref.refs_0_
  28.7 0.0 collective-permute-done.6.got_ref
  28.7 0.1 core_add.1
  28.8 0.7 %collective-permute-start.7 = (bf16[72,768]{1,0:T(8,128)(2,1)S(1)}, bf16[72,768]{1,0:T(8,128)(2,1)S(1)}, u32[]{:S(2)}, u32[]{:S(2)}) collective-permute-start(bf16[72,768]{1,0:T(8,128)(2,1)S(1)} %get-tuple-element.64), channel_id=1, source_target_pairs={{0,4},{1,5},{2,6},{3,7},{4,0},{5,1},{6,2},{7,3},{8,12},{9,13},{10,... | collective-permute-start | bytes 331784 | tf_op jit(solution)/shard_map/ppermute | solution.py:640
  29.5 0.7 %collective-permute-start.8 = (bf16[72,768]{1,0:T(8,128)(2,1)S(1)}, bf16[72,768]{1,0:T(8,128)(2,1)S(1)}, u32[]{:S(2)}, u32[]{:S(2)}) collective-permute-start(bf16[72,768]{1,0:T(8,128)(2,1)S(1)} %get-tuple-element.65), channel_id=1, source_target_pairs={{0,2},{1,3},{2,0},{3,1},{4,6},{5,7},{6,4},{7,5},{8,10},{9,11},{10,... | collective-permute-start | bytes 331784 | tf_op jit(solution)/shard_map/ppermute | solution.py:640
  30.2 2.2 %collective-permute-start.9 = (bf16[72,768]{1,0:T(8,128)(2,1)S(1)}, bf16[72,768]{1,0:T(8,128)(2,1)S(1)}, u32[]{:S(2)}, u32[]{:S(2)}) collective-permute-start(bf16[72,768]{1,0:T(8,128)(2,1)S(1)} %get-tuple-element.66), channel_id=1, source_target_pairs={{0,6},{1,7},{2,4},{3,5},{4,2},{5,3},{6,0},{7,1},{8,14},{9,15},{10,... | collective-permute-start | bytes 331784 | tf_op jit(solution)/shard_map/ppermute | solution.py:640
  32.4 0.0 copy-done.5
  32.4 0.0 copy-done.6
  32.4 1.2 %to_home.1 = (bf16[576,192]{1,0:T(8,128)(2,1)}, f32[1,192]{1,0:T(1,128)S(1)}) custom-call(bf16[112,384]{1,0:T(8,128)(2,1)S(1)} %get-tuple-element.56.own_ref, bf16[112,384]{1,0:T(8,128)(2,1)S(1)} %collective-permute-done.3.north_ref.refs_0_, bf16[40,384]{1,0:T(8,128)(2,1)S(1)} %collective-permute-done.4.side_ref.refs_1_, ...), custom_call_target="tpu_custom_call" | custom-call | flops 127401984 | bytes 4194304 | tf_op jit(solution)/shard_map/to_home/pallas_call | solution.py:493
  33.6 0.9 %collective-permute-done.7.refs_0_ = bf16[72,768]{1,0:T(8,128)(2,1)S(1)} collective-permute-done((bf16[72,768]{1,0:T(8,128)(2,1)S(1)}, bf16[72,768]{1,0:T(8,128)(2,1)S(1)}, u32[]{:S(2)}, u32[]{:S(2)}) %collective-permute-start.7) | collective-permute-done | bytes 110624 | tf_op jit(solution)/shard_map/ppermute | solution.py:640
  34.5 0.2 collective-permute-done.8.refs_1_
  34.7 2.0 %collective-permute-done.9.refs_2_ = bf16[72,768]{1,0:T(8,128)(2,1)S(1)} collective-permute-done((bf16[72,768]{1,0:T(8,128)(2,1)S(1)}, bf16[72,768]{1,0:T(8,128)(2,1)S(1)}, u32[]{:S(2)}, u32[]{:S(2)}) %collective-permute-start.9) | collective-permute-done | bytes 110624 | tf_op jit(solution)/shard_map/ppermute | solution.py:640
  36.7 0.1 chip_add.1.one_ref
  36.8 1.0 %collective-permute-start.10 = (bf16[440,128]{1,0:T(8,128)(2,1)S(1)}, bf16[440,128]{1,0:T(8,128)(2,1)S(1)}, u32[]{:S(2)}, u32[]{:S(2)}) collective-permute-start(bf16[440,128]{1,0:T(8,128)(2,1)S(1)} %chip_add.1.one_ref), channel_id=1, source_target_pairs={{0,8},{1,9},{2,10},{3,11},{4,12},{5,13},{6,14},{7,15},{8,0},{9,1},... | collective-permute-start | bytes 337928 | tf_op jit(solution)/shard_map/ppermute | solution.py:640
  37.8 3.9 %collective-permute-done.10.two_ref = bf16[440,128]{1,0:T(8,128)(2,1)S(1)} collective-permute-done((bf16[440,128]{1,0:T(8,128)(2,1)S(1)}, bf16[440,128]{1,0:T(8,128)(2,1)S(1)}, u32[]{:S(2)}, u32[]{:S(2)}) %collective-permute-start.10) | collective-permute-done | bytes 112672 | tf_op jit(solution)/shard_map/ppermute | solution.py:640
  41.7 2.2 %collective-permute-start.11 = (bf16[440,128]{1,0:T(8,128)(2,1)S(1)}, bf16[440,128]{1,0:T(8,128)(2,1)S(1)}, u32[]{:S(2)}, u32[]{:S(2)}) collective-permute-start(bf16[440,128]{1,0:T(8,128)(2,1)S(1)} %deep_add.2.one_ref), channel_id=1, source_target_pairs={{0,16},{1,17},{2,18},{3,19},{4,20},{5,21},{6,22},{7,23},{8,24},{9,... | collective-permute-start | bytes 337928 | tf_op jit(solution)/shard_map/ppermute | solution.py:640
  43.9 4.7 %collective-permute-done.11.two_ref = bf16[440,128]{1,0:T(8,128)(2,1)S(1)} collective-permute-done((bf16[440,128]{1,0:T(8,128)(2,1)S(1)}, bf16[440,128]{1,0:T(8,128)(2,1)S(1)}, u32[]{:S(2)}, u32[]{:S(2)}) %collective-permute-start.11) | collective-permute-done | bytes 112672 | tf_op jit(solution)/shard_map/ppermute | solution.py:640
  48.7 1.8 %collective-permute-start.14 = (bf16[440,128]{1,0:T(8,128)(2,1)S(1)}, bf16[440,128]{1,0:T(8,128)(2,1)S(1)}, u32[]{:S(2)}, u32[]{:S(2)}) collective-permute-start(bf16[440,128]{1,0:T(8,128)(2,1)S(1)} %deep_add.3.refs_0_), channel_id=1, source_target_pairs={{0,6},{1,7},{2,4},{3,5},{4,2},{5,3},{6,0},{7,1},{8,14},{9,15},{10,... | collective-permute-start | bytes 337928 | tf_op jit(solution)/shard_map/ppermute | solution.py:640
  50.4 1.4 %collective-permute-start.13 = (bf16[440,128]{1,0:T(8,128)(2,1)S(1)}, bf16[440,128]{1,0:T(8,128)(2,1)S(1)}, u32[]{:S(2)}, u32[]{:S(2)}) collective-permute-start(bf16[440,128]{1,0:T(8,128)(2,1)S(1)} %deep_add.3.refs_0_), channel_id=1, source_target_pairs={{0,2},{1,3},{2,0},{3,1},{4,6},{5,7},{6,4},{7,5},{8,10},{9,11},{10,... | collective-permute-start | bytes 337928 | tf_op jit(solution)/shard_map/ppermute | solution.py:640
  51.8 0.4 collective-permute-start.12
  52.2 3.0 %collective-permute-done.14.refs_3_ = bf16[440,128]{1,0:T(8,128)(2,1)S(1)} collective-permute-done((bf16[440,128]{1,0:T(8,128)(2,1)S(1)}, bf16[440,128]{1,0:T(8,128)(2,1)S(1)}, u32[]{:S(2)}, u32[]{:S(2)}) %collective-permute-start.14) | collective-permute-done | bytes 112672 | tf_op jit(solution)/shard_map/ppermute | solution.py:640
  55.2 0.8 %collective-permute-done.13.refs_2_ = bf16[440,128]{1,0:T(8,128)(2,1)S(1)} collective-permute-done((bf16[440,128]{1,0:T(8,128)(2,1)S(1)}, bf16[440,128]{1,0:T(8,128)(2,1)S(1)}, u32[]{:S(2)}, u32[]{:S(2)}) %collective-permute-start.13) | collective-permute-done | bytes 112672 | tf_op jit(solution)/shard_map/ppermute | solution.py:640
  56.0 0.6 %collective-permute-done.12.refs_1_ = bf16[440,128]{1,0:T(8,128)(2,1)S(1)} collective-permute-done((bf16[440,128]{1,0:T(8,128)(2,1)S(1)}, bf16[440,128]{1,0:T(8,128)(2,1)S(1)}, u32[]{:S(2)}, u32[]{:S(2)}) %collective-permute-start.12) | collective-permute-done | bytes 112672 | tf_op jit(solution)/shard_map/ppermute | solution.py:640
  56.6 0.1 join.1.chunks_ref
  56.7 0.1 collective-permute-start.15
  56.8 1.0 %finish_own.1 = (f32[192,576]{1,0:T(8,128)}, f32[192,192]{1,0:T(8,128)}, f32[192,768]{1,0:T(8,128)}, f32[192,768]{1,0:T(8,128)}, f32[1,192]{1,0:T(1,128)S(1)}) custom-call(bf16[1760,128]{1,0:T(8,128)(2,1)S(1)} %join.1.chunks_ref), custom_call_target="tpu_custom_call" | custom-call | flops 1000000 | bytes 2097152 | tf_op jit(solution)/shard_map/finish_own/pallas_call | solution.py:585
  57.8 0.7 %collective-permute-done.15.chunks_ref = bf16[1760,128]{1,0:T(8,128)(2,1)S(1)} collective-permute-done((bf16[1760,128]{1,0:T(8,128)(2,1)S(1)}, bf16[1760,128]{1,0:T(8,128)(2,1)S(1)}, u32[]{:S(2)}, u32[]{:S(2)}) %collective-permute-start.15) | collective-permute-done | bytes 450592 | tf_op jit(solution)/shard_map/ppermute | solution.py:640
  58.5 1.0 %finish_far.1 = (f32[192,576]{1,0:T(8,128)}, f32[192,192]{1,0:T(8,128)}, f32[192,768]{1,0:T(8,128)}, f32[192,768]{1,0:T(8,128)}, f32[1,192]{1,0:T(1,128)}) custom-call(bf16[1760,128]{1,0:T(8,128)(2,1)S(1)} %collective-permute-done.15.chunks_ref, ...), custom_call_target="tpu_custom_call", output_to_operand_aliasing={{0}: (2, {}), {1}: (3, {}), {2}: (4, {}), {3}: (5, {})} | custom-call | flops 1000000 | bytes 2097152 | tf_op jit(solution)/shard_map/finish_far/pallas_call | solution.py:585
  (2 shorter events, 0.1 us)
Async XLA Ops:
  3.2 7.9 %collective-permute-start = (bf16[216,384]{1,0:T(8,128)(2,1)}, bf16[216,384]{1,0:T(8,128)(2,1)S(1)}, u32[]{:S(2)}, u32[]{:S(2)}) collective-permute-start(bf16[216,384]{1,0:T(8,128)(2,1)} %get-tuple-element.43), channel_id=1, source_target_pairs={{0,1},{1,2},{2,3},{3,0},{4,5},{5,6},{6,7},{7,4},{8,9},{9,10},{10,1... | collective-permute-start | bytes 497672 | tf_op jit(solution)/shard_map/ppermute | solution.py:640
  3.7 9.2 %collective-permute-start.1 = (bf16[72,384]{1,0:T(8,128)(2,1)}, bf16[72,384]{1,0:T(8,128)(2,1)S(1)}, u32[]{:S(2)}, u32[]{:S(2)}) collective-permute-start(bf16[72,384]{1,0:T(8,128)(2,1)} %get-tuple-element.44), channel_id=1, source_target_pairs={{0,4},{1,5},{2,6},{3,7},{4,8},{5,9},{6,10},{7,11},{8,12},{9,13},{1... | collective-permute-start | bytes 165896 | tf_op jit(solution)/shard_map/ppermute | solution.py:640
  6.3 7.5 %collective-permute-start.2 = (bf16[72,384]{1,0:T(8,128)(2,1)}, bf16[72,384]{1,0:T(8,128)(2,1)S(1)}, u32[]{:S(2)}, u32[]{:S(2)}) collective-permute-start(bf16[72,384]{1,0:T(8,128)(2,1)} %get-tuple-element.45), channel_id=1, source_target_pairs={{0,5},{1,6},{2,7},{3,4},{4,9},{5,10},{6,11},{7,8},{8,13},{9,14},{1... | collective-permute-start | bytes 165896 | tf_op jit(solution)/shard_map/ppermute | solution.py:640
  8.7 1.0 %copy-start.2 = (f32[1,2,6,144,23]{3,1,4,2,0:T(2,128)S(1)}, f32[1,2,6,144,23]{3,1,4,2,0:T(2,128)}, u32[]{:S(2)}) copy-start(f32[1,2,6,144,23]{3,1,4,2,0:T(2,128)} %param.19) | copy-start | bytes 476932
  9.7 1.4 %copy-start.3 = (bf16[192,576]{1,0:T(8,128)(2,1)S(1)}, bf16[192,576]{1,0:T(8,128)(2,1)}, u32[]{:S(2)}) copy-start(bf16[192,576]{1,0:T(8,128)(2,1)} %refs_5_.1) | copy-start | bytes 663556
  9.7 1.4 %copy-start.4 = (bf16[192,192]{1,0:T(8,128)(2,1)S(1)}, bf16[192,192]{1,0:T(8,128)(2,1)}, u32[]{:S(2)}) copy-start(bf16[192,192]{1,0:T(8,128)(2,1)} %refs_6_.1) | copy-start | bytes 221188
  9.7 1.5 %copy-start.7 = (bf16[216,384]{1,0:T(8,128)(2,1)S(1)}, bf16[216,384]{1,0:T(8,128)(2,1)}, u32[]{:S(2)}) copy-start(bf16[216,384]{1,0:T(8,128)(2,1)} %get-tuple-element.42.own_ref.refs_0_) | copy-start | bytes 497668
  11.1 2.7 %copy-start = (bf16[192,768]{1,0:T(8,128)(2,1)S(1)}, bf16[192,768]{1,0:T(8,128)(2,1)}, u32[]{:S(2)}) copy-start(bf16[192,768]{1,0:T(8,128)(2,1)} %refs_7_.1) | copy-start | bytes 884740
  11.2 2.7 %copy-start.1 = (bf16[768,192]{0,1:T(8,128)(2,1)S(1)}, bf16[768,192]{0,1:T(8,128)(2,1)}, u32[]{:S(2)}) copy-start(bf16[768,192]{0,1:T(8,128)(2,1)} %param.18) | copy-start | bytes 884740
  13.8 18.6 %copy-start.5 = (s32[6,24]{1,0:T(8,128)S(1)}, s32[6,24]{1,0:T(8,128)}, u32[]{:S(2)}) copy-start(s32[6,24]{1,0:T(8,128)} %land_ref.1) | copy-start | bytes 1732
  13.8 18.6 %copy-start.6 = (s32[1,576]{1,0:T(1,128)S(1)}, s32[1,576]{1,0:T(1,128)}, u32[]{:S(2)}) copy-start(s32[1,576]{1,0:T(1,128)} %constant.5.clone.perm_ref) | copy-start | bytes 6916
  21.3 7.4 %collective-permute-start.6 = (bf16[288,768]{1,0:T(8,128)(2,1)S(1)}, bf16[288,768]{1,0:T(8,128)(2,1)S(1)}, u32[]{:S(2)}, u32[]{:S(2)}) collective-permute-start(bf16[288,768]{1,0:T(8,128)(2,1)S(1)} %get-tuple-element.62), channel_id=1, source_target_pairs={{0,1},{1,0},{2,3},{3,2},{4,5},{5,4},{6,7},{7,6},{8,9},{9,8},{10,11... | collective-permute-start | bytes 1327112 | tf_op jit(solution)/shard_map/ppermute | solution.py:640
  21.7 7.1 %collective-permute-start.3 = (bf16[112,384]{1,0:T(8,128)(2,1)S(1)}, bf16[112,384]{1,0:T(8,128)(2,1)S(1)}, u32[]{:S(2)}, u32[]{:S(2)}) collective-permute-start(bf16[112,384]{1,0:T(8,128)(2,1)S(1)} %get-tuple-element.57), channel_id=1, source_target_pairs={{0,3},{1,0},{2,1},{3,2},{4,7},{5,4},{6,5},{7,6},{8,11},{9,8},{10,9... | collective-permute-start | bytes 258056 | tf_op jit(solution)/shard_map/ppermute | solution.py:640
  23.0 3.9 %collective-permute-start.4 = (bf16[40,384]{1,0:T(8,128)(2,1)S(1)}, bf16[40,384]{1,0:T(8,128)(2,1)S(1)}, u32[]{:S(2)}, u32[]{:S(2)}) collective-permute-start(bf16[40,384]{1,0:T(8,128)(2,1)S(1)} %get-tuple-element.58), channel_id=1, source_target_pairs={{0,28},{1,29},{2,30},{3,31},{4,0},{5,1},{6,2},{7,3},{8,4},{9,5},{1... | collective-permute-start | bytes 92168 | tf_op jit(solution)/shard_map/ppermute | solution.py:640
  25.3 3.4 %collective-permute-start.5 = (bf16[40,384]{1,0:T(8,128)(2,1)S(1)}, bf16[40,384]{1,0:T(8,128)(2,1)S(1)}, u32[]{:S(2)}, u32[]{:S(2)}) collective-permute-start(bf16[40,384]{1,0:T(8,128)(2,1)S(1)} %get-tuple-element.59), channel_id=1, source_target_pairs={{0,31},{1,28},{2,29},{3,30},{4,3},{5,0},{6,1},{7,2},{8,7},{9,4},{1... | collective-permute-start | bytes 92168 | tf_op jit(solution)/shard_map/ppermute | solution.py:640
  28.8 5.7 %collective-permute-start.7 = (bf16[72,768]{1,0:T(8,128)(2,1)S(1)}, bf16[72,768]{1,0:T(8,128)(2,1)S(1)}, u32[]{:S(2)}, u32[]{:S(2)}) collective-permute-start(bf16[72,768]{1,0:T(8,128)(2,1)S(1)} %get-tuple-element.64), channel_id=1, source_target_pairs={{0,4},{1,5},{2,6},{3,7},{4,0},{5,1},{6,2},{7,3},{8,12},{9,13},{10,... | collective-permute-start | bytes 331784 | tf_op jit(solution)/shard_map/ppermute | solution.py:640
  29.5 5.2 %collective-permute-start.8 = (bf16[72,768]{1,0:T(8,128)(2,1)S(1)}, bf16[72,768]{1,0:T(8,128)(2,1)S(1)}, u32[]{:S(2)}, u32[]{:S(2)}) collective-permute-start(bf16[72,768]{1,0:T(8,128)(2,1)S(1)} %get-tuple-element.65), channel_id=1, source_target_pairs={{0,2},{1,3},{2,0},{3,1},{4,6},{5,7},{6,4},{7,5},{8,10},{9,11},{10,... | collective-permute-start | bytes 331784 | tf_op jit(solution)/shard_map/ppermute | solution.py:640
  30.2 6.6 %collective-permute-start.9 = (bf16[72,768]{1,0:T(8,128)(2,1)S(1)}, bf16[72,768]{1,0:T(8,128)(2,1)S(1)}, u32[]{:S(2)}, u32[]{:S(2)}) collective-permute-start(bf16[72,768]{1,0:T(8,128)(2,1)S(1)} %get-tuple-element.66), channel_id=1, source_target_pairs={{0,6},{1,7},{2,4},{3,5},{4,2},{5,3},{6,0},{7,1},{8,14},{9,15},{10,... | collective-permute-start | bytes 331784 | tf_op jit(solution)/shard_map/ppermute | solution.py:640
  36.8 4.8 %collective-permute-start.10 = (bf16[440,128]{1,0:T(8,128)(2,1)S(1)}, bf16[440,128]{1,0:T(8,128)(2,1)S(1)}, u32[]{:S(2)}, u32[]{:S(2)}) collective-permute-start(bf16[440,128]{1,0:T(8,128)(2,1)S(1)} %chip_add.1.one_ref), channel_id=1, source_target_pairs={{0,8},{1,9},{2,10},{3,11},{4,12},{5,13},{6,14},{7,15},{8,0},{9,1},... | collective-permute-start | bytes 337928 | tf_op jit(solution)/shard_map/ppermute | solution.py:640
  41.7 6.9 %collective-permute-start.11 = (bf16[440,128]{1,0:T(8,128)(2,1)S(1)}, bf16[440,128]{1,0:T(8,128)(2,1)S(1)}, u32[]{:S(2)}, u32[]{:S(2)}) collective-permute-start(bf16[440,128]{1,0:T(8,128)(2,1)S(1)} %deep_add.2.one_ref), channel_id=1, source_target_pairs={{0,16},{1,17},{2,18},{3,19},{4,20},{5,21},{6,22},{7,23},{8,24},{9,... | collective-permute-start | bytes 337928 | tf_op jit(solution)/shard_map/ppermute | solution.py:640
  48.7 6.5 %collective-permute-start.14 = (bf16[440,128]{1,0:T(8,128)(2,1)S(1)}, bf16[440,128]{1,0:T(8,128)(2,1)S(1)}, u32[]{:S(2)}, u32[]{:S(2)}) collective-permute-start(bf16[440,128]{1,0:T(8,128)(2,1)S(1)} %deep_add.3.refs_0_), channel_id=1, source_target_pairs={{0,6},{1,7},{2,4},{3,5},{4,2},{5,3},{6,0},{7,1},{8,14},{9,15},{10,... | collective-permute-start | bytes 337928 | tf_op jit(solution)/shard_map/ppermute | solution.py:640
  50.4 5.5 %collective-permute-start.13 = (bf16[440,128]{1,0:T(8,128)(2,1)S(1)}, bf16[440,128]{1,0:T(8,128)(2,1)S(1)}, u32[]{:S(2)}, u32[]{:S(2)}) collective-permute-start(bf16[440,128]{1,0:T(8,128)(2,1)S(1)} %deep_add.3.refs_0_), channel_id=1, source_target_pairs={{0,2},{1,3},{2,0},{3,1},{4,6},{5,7},{6,4},{7,5},{8,10},{9,11},{10,... | collective-permute-start | bytes 337928 | tf_op jit(solution)/shard_map/ppermute | solution.py:640
  51.8 4.8 %collective-permute-start.12 = (bf16[440,128]{1,0:T(8,128)(2,1)S(1)}, bf16[440,128]{1,0:T(8,128)(2,1)S(1)}, u32[]{:S(2)}, u32[]{:S(2)}) collective-permute-start(bf16[440,128]{1,0:T(8,128)(2,1)S(1)} %deep_add.3.refs_0_), channel_id=1, source_target_pairs={{0,4},{1,5},{2,6},{3,7},{4,0},{5,1},{6,2},{7,3},{8,12},{9,13},{10,... | collective-permute-start | bytes 337928 | tf_op jit(solution)/shard_map/ppermute | solution.py:640
  56.7 1.9 %collective-permute-start.15 = (bf16[1760,128]{1,0:T(8,128)(2,1)S(1)}, bf16[1760,128]{1,0:T(8,128)(2,1)S(1)}, u32[]{:S(2)}, u32[]{:S(2)}) collective-permute-start(bf16[1760,128]{1,0:T(8,128)(2,1)S(1)} %join.1.chunks_ref), channel_id=1, source_target_pairs={{0,1},{1,0},{2,3},{3,2},{4,5},{5,4},{6,7},{7,6},{8,9},{9,8},{10,11... | collective-permute-start | bytes 1351688 | tf_op jit(solution)/shard_map/ppermute | solution.py:640
